TPU v7x, 128 devices: a whole 4x4x4 slice. The times are simulated.
128 devices in a mesh: dp: 32 (over z, x, y_lo), seq: 4 (over y_hi, core).
Axes of the slice: x: 4, y: 4 (y_hi: 2, y_lo: 2; y = y_hi * 2 + y_lo), z: 4, core: 2. Of those that a mesh axis runs over, the one named last changes fastest.
Arguments:
- tokens: bfloat16 [32, 1024, 1024], P('dp', 'seq'), may hold values from -15 to 15
- lengths: int32 [32, 4], P('dp'), may hold values from 1 to 1021, as said below
- ln_gain: bfloat16 [1024], replicated, may hold values from 0.5 to 1.5
- ln_bias: bfloat16 [1024], replicated, may hold values from -3 to 3
- w_qkv: bfloat16 [1024, 3072], replicated, may hold values from -0.1875 to 0.1875
- b_qkv: bfloat16 [3072], replicated, may hold values from -3 to 3
- w_out: bfloat16 [1024, 1024], replicated, may hold values from -1.5 to 1.5
- b_out: bfloat16 [1024], replicated, may hold values from -3 to 3
- w_in: bfloat16 [1024, 4096], replicated, may hold values from -0.1875 to 0.1875
- b_in: bfloat16 [4096], replicated, may hold values from -3 to 3
- w_down: bfloat16 [4096, 1024], replicated, may hold values from -0.09375 to 0.09375
- b_down: bfloat16 [1024], replicated, may hold values from -3 to 3
- cotangent: bfloat16 [32, 1024, 1024], P('dp', 'seq'), may hold values from -6 to 6
Outputs:
- output: bfloat16 [32, 1024, 1024], P('dp', 'seq')
- grad_tokens: float32 [32, 1024, 1024], P('dp', 'seq')
- grad_ln_gain: float32 [1024], P(('dp', 'seq'))
- grad_ln_bias: float32 [1024], P(('dp', 'seq'))
- grad_w_qkv: float32 [1024, 3072], P(('dp', 'seq'))
- grad_b_qkv: float32 [3072], P(('dp', 'seq'))
- grad_w_out: float32 [1024, 1024], P(('dp', 'seq'))
- grad_b_out: float32 [1024], P(('dp', 'seq'))
- grad_w_in: float32 [1024, 4096], P(('dp', 'seq'))
- grad_b_in: float32 [4096], P(('dp', 'seq'))
- grad_w_down: float32 [4096, 1024], P(('dp', 'seq'))
- grad_b_down: float32 [1024], P(('dp', 'seq'))
Inputs may be any that keep to these rules, and one draw needn't show every extreme that they name: Each row's lengths sum to 1024. In each row one document, at a drawn place, starts within the first 256 slots and ends within the last 256; every other document has at most 64 slots.
All inputs are finite; a program needn't handle non-finite values.
Results may differ from a plain program's by a relative error of at most 0.0087.
Values may be sent and summed in bfloat16 or wider, within the bound.
A program may use at most 192 MiB of HBM per device.

v0:
```python
from functools import partial
import math

import jax
import jax.numpy as jnp
from jax import lax
from jax.sharding import PartitionSpec as P

HEADS = 16
HEAD = 64
ROT = 16


def layer_norm(inputs, gain_vec, shift_add):
    centre = inputs - jnp.mean(inputs, axis=-1, keepdims=True)
    spread = jnp.mean(centre * centre, axis=-1, keepdims=True)
    return centre * lax.rsqrt(spread + 1e-05) * gain_vec + shift_add


def gelu_exact(values):
    return jax.nn.gelu(values, approximate=False)


def rotary(values_in, places):
    half_dims = ROT // 2
    freq_steps = jnp.arange(half_dims, dtype=jnp.float32)
    inverse = jnp.exp(freq_steps * (-2.0 * math.log(10000.0) / ROT))
    angles = places[:, None] * inverse[None, :]
    cosine = jnp.cos(angles)[:, None, :]
    sine = jnp.sin(angles)[:, None, :]
    first_half = values_in[..., :half_dims]
    second_half = values_in[..., half_dims:ROT]
    return jnp.concatenate(
        [
            first_half * cosine - second_half * sine,
            second_half * cosine + first_half * sine,
            values_in[..., ROT:],
        ],
        axis=-1,
    )


def doc_layout(lengths_row, places):
    doc_ends = jnp.cumsum(lengths_row)
    doc_starts = doc_ends - lengths_row
    inside = (places[:, None] >= doc_starts[None, :]) & (places[:, None] < doc_ends[None, :])
    member = inside.astype(jnp.int32)
    doc_ids = jnp.sum(member * jnp.arange(lengths_row.shape[0], dtype=jnp.int32)[None, :], axis=1)
    offsets = places - jnp.sum(member * doc_starts[None, :], axis=1)
    return (doc_ids, offsets)


def contract_rows(left, right):
    return lax.dot_general(
        left, right, (((0,), (0,)), ((), ())), preferred_element_type=jnp.float32
    )


def contract_cols(left, right):
    return lax.dot_general(
        left, right, (((1,), (1,)), ((), ())), preferred_element_type=jnp.float32
    )


def on_device(
    tokens,
    lengths,
    ln_gain,
    ln_bias,
    w_qkv,
    b_qkv,
    w_out,
    b_out,
    w_in,
    b_in,
    w_down,
    b_down,
    cotangent,
):
    tok_count = tokens.shape[1]
    seq_groups = lax.axis_size("seq")
    shard_index = lax.axis_index("seq")
    model_width = w_qkv.shape[0]
    row_len = tok_count * seq_groups
    local_heads = HEADS // seq_groups
    score_scale = 1.0 / math.sqrt(HEAD)
    row_lengths = lengths[0]
    own_slots = shard_index * tok_count + jnp.arange(tok_count, dtype=jnp.int32)
    places = doc_layout(row_lengths, own_slots)[1].astype(jnp.float32)
    row_slots = jnp.arange(row_len, dtype=jnp.int32)
    row_docs = doc_layout(row_lengths, row_slots)[0]
    inputs = tokens[0].astype(jnp.float32)
    normed32, ln_back = jax.vjp(
        layer_norm, inputs, ln_gain.astype(jnp.float32), ln_bias.astype(jnp.float32)
    )
    normed = normed32.astype(jnp.bfloat16)
    project = jnp.dot(normed, w_qkv, preferred_element_type=jnp.float32) + b_qkv.astype(jnp.float32)
    pre_query = project[:, :model_width].reshape(tok_count, HEADS, HEAD)
    pre_key = project[:, model_width : 2 * model_width].reshape(tok_count, HEADS, HEAD)
    query_rot, rotary_back = jax.vjp(partial(rotary, places=places), pre_query)
    key_rot = rotary(pre_key, places)
    query_tok = query_rot.reshape(tok_count, model_width).astype(jnp.bfloat16)
    key_tok = key_rot.reshape(tok_count, model_width).astype(jnp.bfloat16)
    value_tok = project[:, 2 * model_width :].astype(jnp.bfloat16)
    query_h, key_h, value_h = (
        lax.all_to_all(query_tok, "seq", split_axis=1, concat_axis=0, tiled=True),
        lax.all_to_all(key_tok, "seq", split_axis=1, concat_axis=0, tiled=True),
        lax.all_to_all(value_tok, "seq", split_axis=1, concat_axis=0, tiled=True),
    )
    query_h = query_h.reshape(row_len, local_heads, HEAD)
    key_h = key_h.reshape(row_len, local_heads, HEAD)
    value_h = value_h.reshape(row_len, local_heads, HEAD)
    block_rows = math.gcd(row_len, 512)
    block_count = row_len // block_rows

    def block_scores(query_blk, first_row):
        rows_here = first_row + jnp.arange(block_rows, dtype=jnp.int32)
        docs_here = lax.dynamic_slice_in_dim(row_docs, first_row, block_rows)
        allowed = (docs_here[:, None] == row_docs[None, :]) & (
            row_slots[None, :] <= rows_here[:, None]
        )
        scores = (
            jnp.einsum("qhd,khd->hqk", query_blk, key_h, preferred_element_type=jnp.float32)
            * score_scale
        )
        return jnp.where(allowed[None], scores, -jnp.inf)

    def forward_block(block_index):
        first_row = block_index * block_rows
        query_blk = lax.dynamic_slice_in_dim(query_h, first_row, block_rows)
        scores = block_scores(query_blk, first_row)
        row_max = jnp.max(scores, axis=-1, keepdims=True)
        exp_scores = jnp.exp(scores - row_max)
        exp_total = jnp.sum(exp_scores, axis=-1, keepdims=True)
        probability = (exp_scores / exp_total).astype(jnp.bfloat16)
        mixed_blk = jnp.einsum(
            "hqk,khd->qhd", probability, value_h, preferred_element_type=jnp.float32
        )
        return (mixed_blk.astype(jnp.bfloat16), (row_max + jnp.log(exp_total))[..., 0])

    mixed_blocks, log_totals = lax.map(forward_block, jnp.arange(block_count, dtype=jnp.int32))
    mixed_h = mixed_blocks.reshape(row_len, local_heads * HEAD)
    mixed_tok = lax.all_to_all(mixed_h, "seq", split_axis=0, concat_axis=1, tiled=True)
    attn_out = jnp.dot(mixed_tok, w_out, preferred_element_type=jnp.float32) + b_out.astype(
        jnp.float32
    )
    hidden = jnp.dot(normed, w_in, preferred_element_type=jnp.float32) + b_in.astype(jnp.float32)
    active32, gelu_back = jax.vjp(gelu_exact, hidden)
    active = active32.astype(jnp.bfloat16)
    ffn_out = jnp.dot(active, w_down, preferred_element_type=jnp.float32) + b_down.astype(
        jnp.float32
    )
    output = (inputs + attn_out + ffn_out).astype(jnp.bfloat16)
    grad_low = cotangent[0]
    grad_top = grad_low.astype(jnp.float32)
    grad_w_out = contract_rows(mixed_tok, grad_low)
    grad_b_out = jnp.sum(grad_top, axis=0)
    grad_w_down = contract_rows(active, grad_low)
    grad_b_down = jnp.sum(grad_top, axis=0)
    grad_active = contract_cols(grad_low, w_down)
    grad_hidden = gelu_back(grad_active)[0].astype(jnp.bfloat16)
    grad_w_in = contract_rows(normed, grad_hidden)
    grad_b_in = jnp.sum(grad_hidden.astype(jnp.float32), axis=0)
    grad_mixed = contract_cols(grad_low, w_out).astype(jnp.bfloat16)
    grad_mixed_h = lax.all_to_all(
        grad_mixed, "seq", split_axis=1, concat_axis=0, tiled=True
    ).reshape(row_len, local_heads, HEAD)

    def backward_block(carry, block_index):
        grad_key, grad_value = carry
        first_row = block_index * block_rows
        query_blk = lax.dynamic_slice_in_dim(query_h, first_row, block_rows)
        grad_blk = lax.dynamic_slice_in_dim(grad_mixed_h, first_row, block_rows)
        log_blk = lax.dynamic_index_in_dim(log_totals, block_index, 0, False)
        scores = block_scores(query_blk, first_row)
        probability = jnp.exp(scores - log_blk[..., None])
        grad_probs = jnp.einsum(
            "qhd,khd->hqk", grad_blk, value_h, preferred_element_type=jnp.float32
        )
        row_inner = jnp.sum(probability * grad_probs, axis=-1, keepdims=True)
        grad_scores = (probability * (grad_probs - row_inner)).astype(jnp.bfloat16)
        grad_query = (
            jnp.einsum("hqk,khd->qhd", grad_scores, key_h, preferred_element_type=jnp.float32)
            * score_scale
        )
        grad_key = (
            grad_key
            + jnp.einsum("hqk,qhd->khd", grad_scores, query_blk, preferred_element_type=jnp.float32)
            * score_scale
        )
        grad_value = grad_value + jnp.einsum(
            "hqk,qhd->khd",
            probability.astype(jnp.bfloat16),
            grad_blk,
            preferred_element_type=jnp.float32,
        )
        return ((grad_key, grad_value), grad_query.astype(jnp.bfloat16))

    zero_heads = jnp.zeros((row_len, local_heads, HEAD), jnp.float32)
    key_value_grads, query_grads = lax.scan(
        backward_block, (zero_heads, zero_heads), jnp.arange(block_count, dtype=jnp.int32)
    )
    grad_query_h = query_grads.reshape(row_len, local_heads * HEAD)
    grad_key_h = key_value_grads[0].reshape(row_len, local_heads * HEAD).astype(jnp.bfloat16)
    grad_value_h = key_value_grads[1].reshape(row_len, local_heads * HEAD).astype(jnp.bfloat16)
    grad_query_tok, grad_key_tok, grad_value_tok = (
        lax.all_to_all(grad_query_h, "seq", split_axis=0, concat_axis=1, tiled=True),
        lax.all_to_all(grad_key_h, "seq", split_axis=0, concat_axis=1, tiled=True),
        lax.all_to_all(grad_value_h, "seq", split_axis=0, concat_axis=1, tiled=True),
    )
    grad_pre_query = rotary_back(
        grad_query_tok.astype(jnp.float32).reshape(tok_count, HEADS, HEAD)
    )[0]
    grad_pre_key = rotary_back(grad_key_tok.astype(jnp.float32).reshape(tok_count, HEADS, HEAD))[0]
    grad_project = jnp.concatenate(
        [
            grad_pre_query.reshape(tok_count, model_width),
            grad_pre_key.reshape(tok_count, model_width),
            grad_value_tok.astype(jnp.float32),
        ],
        axis=1,
    ).astype(jnp.bfloat16)
    grad_w_qkv = contract_rows(normed, grad_project)
    grad_b_qkv = jnp.sum(grad_project.astype(jnp.float32), axis=0)
    grad_normed = contract_cols(grad_project, w_qkv) + contract_cols(grad_hidden, w_in)
    grad_input, grad_ln_gain, grad_ln_bias = ln_back(grad_normed)
    grad_tokens = (grad_top + grad_input)[None]
    summed = (
        lax.psum_scatter(grad_ln_gain, ("dp", "seq"), scatter_dimension=0, tiled=True),
        lax.psum_scatter(grad_ln_bias, ("dp", "seq"), scatter_dimension=0, tiled=True),
        lax.psum_scatter(grad_w_qkv, ("dp", "seq"), scatter_dimension=0, tiled=True),
        lax.psum_scatter(grad_b_qkv, ("dp", "seq"), scatter_dimension=0, tiled=True),
        lax.psum_scatter(grad_w_out, ("dp", "seq"), scatter_dimension=0, tiled=True),
        lax.psum_scatter(grad_b_out, ("dp", "seq"), scatter_dimension=0, tiled=True),
        lax.psum_scatter(grad_w_in, ("dp", "seq"), scatter_dimension=0, tiled=True),
        lax.psum_scatter(grad_b_in, ("dp", "seq"), scatter_dimension=0, tiled=True),
        lax.psum_scatter(grad_w_down, ("dp", "seq"), scatter_dimension=0, tiled=True),
        lax.psum_scatter(grad_b_down, ("dp", "seq"), scatter_dimension=0, tiled=True),
    )
    return (
        output[None],
        grad_tokens,
        summed[0],
        summed[1],
        summed[2],
        summed[3],
        summed[4],
        summed[5],
        summed[6],
        summed[7],
        summed[8],
        summed[9],
    )


def solution(mesh):
    return jax.shard_map(
        on_device,
        mesh=mesh,
        in_specs=(
            P("dp", "seq", None),
            P("dp", None),
            P(),
            P(),
            P(),
            P(),
            P(),
            P(),
            P(),
            P(),
            P(),
            P(),
            P("dp", "seq", None),
        ),
        out_specs=(
            P("dp", "seq", None),
            P("dp", "seq", None),
            P(("dp", "seq")),
            P(("dp", "seq")),
            P(("dp", "seq"), None),
            P(("dp", "seq")),
            P(("dp", "seq"), None),
            P(("dp", "seq")),
            P(("dp", "seq"), None),
            P(("dp", "seq")),
            P(("dp", "seq"), None),
            P(("dp", "seq")),
        ),
        check_vma=False,
    )
```

profile of v0, /device:TPU:1, one launch (start us, length us, event | category | flops | bytes accessed | tf_op | source)
XLA Modules:
  0.0 2763.4 jit_solution(5627351679035694917)
XLA Ops:
  12.0 4.9 convolution_add_fusion.1
  28.5 15.2 all_to_all.110
  43.6 4.5 all-to-all-start.1
  52.1 5.5 all-to-all-done.1
  57.6 5.0 all-to-all-start.2
  66.6 5.5 all-to-all-done.2
  72.2 4.8 all-to-all-start.4
  82.1 22.3 while.28
  112.4 4.8 all-to-all-start.3
  121.7 5.0 all-to-all-done.3
  131.5 65.4 %while.29 = (s32[]{:T(128)}, f32[1024,4,64]{0,2,1:T(8,128)}, f32[1024,4,64]{0,2,1:T(8,128)}, bf16[2,512,4,64]{1,3,2,0:T(8,128)(2,1)}, s32[2]{0:T(128)S(1)}, /*in...) while((s32[]{:T(128)}, f32[1024,4,64]{0,2,1:T(8,128)}, ...), condition=%wide.region_11.12_spmd.clone, body=%wide.region_9.11_spmd.clone.sunk | while | flops 1376778752 | bytes 132979592 | solution.py:200
  133.4 5.5 fusion.146
  140.9 6.9 multiply_reduce_fusion.2
  165.4 5.5 fusion.146
  172.9 6.9 multiply_reduce_fusion.2
  183.5 4.5 fusion.148
  204.1 5.4 all-to-all-start.5
  212.8 7.0 all-to-all-done.5
  233.6 5.1 all-to-all-start.7
  240.9 7.9 all-to-all-done.7
  248.8 7.7 fusion.79
  257.2 14.8 multiply_convert_fusion.1
  272.1 7.3 convert_reduce_fusion
  280.8 8.3 fusion.81
  289.3 9.8 fusion.67
  299.8 6.5 fusion.89
  306.4 6.9 convolution_add_fusion.4
  320.1 67.5 %all-reduce.11 = (f32[1024]{0:T(1024)S(1)}, f32[1024]{0:T(1024)S(1)}, f32[3072]{0:T(1024)S(1)}, f32[1024]{0:T(1024)S(1)}, f32[4096]{0:T(1024)S(1)}) all-reduce(f32[1024]{0:T(1024)S(1)} %get-tuple-element.204, f32[1024]{0:T(1024)S(1)} %get-tuple-element.206, ...), channel_id=2, replica_groups=mesh['dp'=32,'seq'=4] {'dp','seq'}, use_global_device_ids=true, to_apply=%region_15.16.clone | all-reduce | flops 10240 | bytes 81920
  392.8 375.0 %reduce-scatter.7.cloned.1.call-done = f32[8,1024]{1,0:T(8,128)} async-done(((f32[1024,1024]{1,0:T(8,128)}), f32[8,1024]{1,0:T(8,128)}) %reduce-scatter.7.cloned.1.call-update) | async-done | bytes 32784 | tf_op jit(solution)/shard_map/reduce_scatter | solution.py:233
  767.8 656.7 %reduce-scatter.5.cloned.1.call-done = f32[8,3072]{1,0:T(8,128)} async-done(((f32[1024,3072]{1,0:T(8,128)}), f32[8,3072]{1,0:T(8,128)}) %reduce-scatter.5.cloned.1.call-update) | async-done | bytes 98320 | tf_op jit(solution)/shard_map/reduce_scatter | solution.py:231
  1424.5 665.8 %reduce-scatter.9.cloned.1.call-done = f32[8,4096]{1,0:T(8,128)} async-done(((f32[1024,4096]{1,0:T(8,128)}), f32[8,4096]{1,0:T(8,128)}) %reduce-scatter.9.cloned.1.call-update) | async-done | bytes 131088 | tf_op jit(solution)/shard_map/reduce_scatter | solution.py:235
  2090.2 666.0 %reduce-scatter.11.cloned.1.call-done = f32[32,1024]{1,0:T(8,128)} async-done(((f32[4096,1024]{1,0:T(8,128)}), f32[32,1024]{1,0:T(8,128)}) %reduce-scatter.11.cloned.1.call-update) | async-done | bytes 131088 | tf_op jit(solution)/shard_map/reduce_scatter | solution.py:237
  (214 shorter events, 140.2 us)
Async XLA Ops:
  7.2 55.4 %copy-start = (bf16[1024,1024]{1,0:T(8,128)(2,1)S(1)}, bf16[1024,1024]{1,0:T(8,128)(2,1)}, u32[]{:S(2)}) copy-start(bf16[1024,1024]{1,0:T(8,128)(2,1)} %param.23) | copy-start | bytes 6291460
  8.6 8.3 copy-start.22
  9.9 7.0 copy-start.24
  26.1 36.4 %copy-start.8 = (bf16[1,256,1024]{2,1,0:T(8,128)(2,1)S(1)}, bf16[1,256,1024]{2,1,0:T(8,128)(2,1)}, u32[]{:S(2)}) copy-start(bf16[1,256,1024]{2,1,0:T(8,128)(2,1)} %param.29) | copy-start | bytes 1572868
  43.6 14.0 all-to-all-start.1
  57.6 14.6 all-to-all-start.2
  72.2 39.4 %all-to-all-start.4 = ((bf16[256,4,256]{2,0,1:T(8,128)(2,1)}), bf16[256,4,256]{2,0,1:T(8,128)(2,1)S(1)}, u32[]{:S(2)}, u32[]{:S(2)}) async-start(bf16[256,4,256]{2,0,1:T(8,128)(2,1)} %bitcast.162), calls=%async_computation.4 | async-start | bytes 1048576 | tf_op jit(solution)/shard_map/all_to_all | solution.py:165
  112.4 14.3 all-to-all-start.3
  117.2 650.6 %reduce-scatter.7.cloned.1.call-start = ((), (), s32[]{:S(2)}) async-start(), calls=%async_computation.13 | async-start | bytes 4227072 | tf_op jit(solution)/shard_map/reduce_scatter | solution.py:233
  151.4 8.6 copy-start.1
  172.9 6.9 slice-start
  183.5 8.9 copy-start.1
  196.9 12.7 copy-start.2
  204.1 15.6 all-to-all-start.5
  219.8 13.8 all-to-all-start.6
  226.6 12.3 copy-start.27
  226.6 12.3 copy-start.29
  231.6 17.2 copy-start.3
  231.6 17.2 copy-start.19
  231.6 17.2 copy-start.21
  231.6 17.2 copy-start.23
  231.6 17.2 copy-start.25
  233.6 15.2 all-to-all-start.7
  238.7 1185.7 %reduce-scatter.5.cloned.1.call-start = ((), (), s32[]{:S(2)}) async-start(), calls=%async_computation.12 | async-start | bytes 12681216 | tf_op jit(solution)/shard_map/reduce_scatter | solution.py:231
  256.6 1833.7 %reduce-scatter.9.cloned.1.call-start = ((), (), s32[]{:S(2)}) async-start(), calls=%async_computation.14 | async-start | bytes 16908288 | tf_op jit(solution)/shard_map/reduce_scatter | solution.py:235
  257.2 14.8 copy-start.9
  289.1 2467.1 %reduce-scatter.11.cloned.1.call-start = ((), (), s32[]{:S(2)}) async-start(), calls=%async_computation.15 | async-start | bytes 16908288 | tf_op jit(solution)/shard_map/reduce_scatter | solution.py:237
  299.8 15.0 slice-start.2
  306.4 6.9 copy-start.7
  306.4 8.4 slice-start.3
  318.0 72.0 %copy-start.5 = (bf16[4,256,256]{1,2,0:T(8,128)(2,1)S(1)}, bf16[4,256,256]{1,2,0:T(8,128)(2,1)}, u32[]{:S(2)}) copy-start(bf16[4,256,256]{1,2,0:T(8,128)(2,1)} %copy-done.4) | copy-start | bytes 1572868
  387.7 2369.0 %copy-start.36 = (f32[8]{0:T(128)}, f32[8]{0:T(128)S(1)}, u32[]{:S(2)}) copy-start(f32[8]{0:T(128)S(1)} %dynamic-slice.3) | copy-start | bytes 100
  (24 other events, 77.3 us)
Sparse Core Ops, SparseCore 0:
  130.7 637.0 reduce-scatter.6
  770.9 653.5 reduce-scatter.4
  1427.4 662.7 reduce-scatter.8
  2093.0 663.1 reduce-scatter.10
where the time goes:
time: 2780 us; the launch traced here: 2760 us
  waiting for transfers between devices  2400 us (86%)
  matrix products  141 us (5%)
  blocking collectives  82.7 us (3%)
  local copies, waits for them, and re-layouts  57.4 us (2%)
  starting transfers between devices  34.3 us (1%)
  other arithmetic  30.7 us (1%)
    reduce_scatter x1, waiting for transfers between devices, on_device(): lax.psum_scatter(grad_w_down, ('dp', 'seq'), scatter_dimension=0, tiled=T...  666 us
    reduce_scatter x1, waiting for transfers between devices, on_device(): lax.psum_scatter(grad_w_in, ('dp', 'seq'), scatter_dimension=0, tiled=True)  666 us
    reduce_scatter x1, waiting for transfers between devices, on_device(): lax.psum_scatter(grad_w_qkv, ('dp', 'seq'), scatter_dimension=0, tiled=True)  657 us
    reduce_scatter x1, waiting for transfers between devices, on_device(): lax.psum_scatter(grad_w_out, ('dp', 'seq'), scatter_dimension=0, tiled=True)  375 us
    unnamed x1, blocking collectives  67.5 us
  transfers between devices with their start and end apart: 11, of which 10 were waited for; matrix products, arithmetic and copies ran while one was open for 7% of the time, Pallas kernels for 0%

commit v1 on v0

v1 whole, which is shorter than its diff:
```python
import math

import jax
import jax.numpy as jnp
from jax import lax
from jax.experimental import pallas as pl
from jax.experimental.pallas import tpu as pltpu
from jax.sharding import PartitionSpec as P

HEAD = 64
ROT = 16
ROW = 1024
D = 1024
BLK = 256
BF = jnp.bfloat16
F32 = jnp.float32
MESH = pl.DeviceIdType.MESH
VMEM_LIMIT = 60 * 2**20


def dot_nn(a, b):
    return lax.dot_general(a, b, (((1,), (0,)), ((), ())), preferred_element_type=F32)


def dot_nt(a, b):
    return lax.dot_general(a, b, (((1,), (1,)), ((), ())), preferred_element_type=F32)


def dot_tn(a, b):
    return lax.dot_general(a, b, (((0,), (0,)), ((), ())), preferred_element_type=F32)


def loop(count, step):
    def run(i, carry):
        step(i)
        return carry

    lax.fori_loop(0, count, run, 0)


def at256(i):
    return pl.ds(pl.multiple_of(i * 256, 256), 256)


SCRATCH = [
    ("win", (D, 1024), BF),
    ("wdn", (1024, D), BF),
    ("wqkv", (D, 768), BF),
    ("wout", (BLK, D), BF),
    ("nall", (ROW, D), BF),
    ("call", (ROW, D), BF),
    ("q", (ROW, BLK), BF),
    ("k", (ROW, BLK), BF),
    ("v", (ROW, BLK), BF),
    ("do", (ROW, BLK), BF),
    ("act", (ROW, 1024), BF),
    ("gh", (ROW, 1024), BF),
    ("g_ffn", (2, 4, 2, 4, 32, 1024), BF),
    ("g_qkv", (4, 2, 4, 32, 768), BF),
    ("g_out", (4, 2, 4, 8, 1024), F32),
    ("outp", (ROW, D), F32),
    ("gnp", (ROW, D), F32),
    ("hid", (256, 256), F32),
    ("ga", (256, 256), F32),
    ("sc", (BLK, ROW), F32),
    ("dp", (BLK, ROW), F32),
    ("bias", (BLK, ROW), F32),
    ("pb", (BLK, ROW), BF),
    ("ds", (BLK, ROW), BF),
    ("dk", (ROW, BLK), F32),
    ("dv", (ROW, BLK), F32),
    ("dq", (BLK, BLK), F32),
    ("mx", (BLK, BLK), F32),
    ("mixed", (ROW, BLK), BF),
    ("gp", (ROW, 768), BF),
    ("tab", (3, ROW, 128), F32),
    ("sm", (4, 8, 1024), F32),
    ("smr", (10, 8, 1024), F32),
    ("rxs", (2, 2, BLK, D), BF),
    ("rxp", (2, BLK, D), BF),
    ("r1_ffn", (2, 6, 2, 4, 32, 512), BF),
    ("r2_ffn", (2, 6, 2, 32, 512), BF),
    ("ry_ffn", (2, 32, 1024), BF),
    ("r1_qkv", (2, 6, 4, 32, 384), BF),
    ("r2_qkv", (2, 6, 32, 384), BF),
    ("ry_qkv", (32, 768), BF),
    ("r1_out", (2, 6, 4, 8, 512), F32),
    ("r2_out", (2, 6, 8, 512), F32),
    ("ry_out", (8, 1024), F32),
    ("fin_in", (32, 1024), F32),
    ("fin_dn", (32, 1024), F32),
    ("fin_qkv", (32, 768), F32),
    ("fin_out", (8, 1024), F32),
]
NSEM = 160
NLOC = 8


class Links:
    def __init__(self, send, recv):
        self.send, self.recv, self.count = send, recv, 0

    def copy(self, src, dst, device):
        k = self.count
        self.count += 1
        return pltpu.make_async_remote_copy(
            src_ref=src,
            dst_ref=dst,
            send_sem=self.send.at[k],
            recv_sem=self.recv.at[k],
            device_id=device,
            device_id_type=MESH,
        )


def add_into(dst, sources):
    if len(dst.shape) > 2:
        for i in range(dst.shape[0]):
            add_into(dst.at[i], [s.at[i] for s in sources])
        return
    total = dst[...].astype(F32)
    for s in sources:
        total = total + s[...].astype(F32)
    dst[...] = total.astype(dst.dtype)


class Ring:
    def __init__(self, links, block, pos, right, left, land):
        self.block, self.land = block, land
        self.pos = pos
        self.rt, self.lf, self.opp = (pos + 1) % 4, (pos + 3) % 4, (pos + 2) % 4
        c = links.copy
        self.early = [
            c(block(self.opp, 0), land.at[0], right),
            c(block(self.opp, 1), land.at[1], left),
            c(block(self.rt, 1), land.at[2], right),
            c(block(self.lf, 0), land.at[3], left),
        ]
        self.late = [
            c(block(self.rt, 0), land.at[4], right),
            c(block(self.lf, 1), land.at[5], left),
        ]

    def start(self):
        for c in self.early:
            c.start()

    def middle(self):
        self.early[0].wait_recv()
        add_into(self.block(self.rt, 0), [self.land.at[0]])
        self.late[0].start()
        self.early[1].wait_recv()
        add_into(self.block(self.lf, 1), [self.land.at[1]])
        self.late[1].start()

    def finish(self):
        for c in self.early[2:] + self.late:
            c.wait_recv()
        add_into(self.block(self.pos, 0), [self.land.at[4], self.land.at[3]])
        add_into(self.block(self.pos, 1), [self.land.at[2], self.land.at[5]])
        for c in self.early + self.late:
            c.wait_send()


class Reduce:
    def __init__(self, links, ref, lead, land1, land2, land_y, where):
        z, x, yl, dev = where["z"], where["x"], where["yl"], where["dev"]
        half = ref.shape[-1] // 2
        pre = (slice(None),) * lead
        every = slice(None)
        first, second = pl.ds(0, half), pl.ds(half, half)

        def view(a, h, b, cols):
            return ref.at[pre + (a, h, b, every, cols)]

        zr, zl = dev(z + 1, x, yl), dev(z + 3, x, yl)
        xr, xl = dev(z, x + 1, yl), dev(z, x + 3, yl)
        self.one = [
            Ring(links, lambda t, h: view(every, h, t, first), z, zr, zl, land1.at[0]),
            Ring(links, lambda t, h: view(t, h, every, second), x, xr, xl, land1.at[1]),
        ]
        self.two = [
            Ring(links, lambda t, h: view(t, h, z, first), x, xr, xl, land2.at[0]),
            Ring(links, lambda t, h: view(x, h, t, second), z, zr, zl, land2.at[1]),
        ]
        self.own = ref.at[pre + (x, yl, z)]
        self.land_y = land_y
        self.y = links.copy(ref.at[pre + (x, 1 - yl, z)], land_y, dev(z, x, 1 - yl))

    def steps(self):
        one, two = self.one, self.two
        return [
            lambda: [r.start() for r in one],
            lambda: [r.middle() for r in one],
            lambda: [r.finish() for r in one] + [r.start() for r in two],
            lambda: [r.middle() for r in two],
            lambda: [r.finish() for r in two] + [self.y.start()],
            lambda: self.y.wait(),
        ]


def kernel(*refs):
    (vecs, lens, tokens, cot, w_qkv, w_out, w_in, w_down) = refs[:8]
    (o_out, o_tok, o_wqkv, o_wout, o_win, o_wdn, o_small) = refs[8:15]
    rest = refs[15:]
    R = {name: r for (name, _, _), r in zip(SCRATCH, rest)}
    send, recv, loc = rest[len(SCRATCH) :]
    links = Links(send, recv)

    dpi, s = lax.axis_index("dp"), lax.axis_index("seq")
    z, x, yl = dpi // 8, (dpi // 2) % 4, dpi % 2
    yh, c = s // 2, s % 2

    def dev(zz, xx, yy):
        return ((zz % 4) * 8 + (xx % 4) * 2 + yy, s)

    where = {"z": z, "x": x, "yl": yl, "dev": dev}
    sibling = (dpi, yh * 2 + 1 - c)
    partner = (dpi, (1 - yh) * 2 + c)
    others = [(dpi, (s + d) % 4) for d in (1, 2, 3)]
    swapped = (s * 8 + x * 2 + yl, z)

    loads = [
        pltpu.make_async_copy(w_qkv.at[:, pl.ds(pl.multiple_of(j * 1024 + s * 256, 256), 256)], R["wqkv"].at[:, pl.ds(j * 256, 256)], loc.at[j])
        for j in range(3)
    ]
    loads.append(pltpu.make_async_copy(w_out.at[at256(s), :], R["wout"], loc.at[3]))
    wide = pl.ds(pl.multiple_of(s * 1024, 1024), 1024)
    loads.append(pltpu.make_async_copy(w_in.at[:, wide], R["win"], loc.at[4]))
    loads.append(pltpu.make_async_copy(w_down.at[wide, :], R["wdn"], loc.at[5]))
    for c_ in loads:
        c_.start()

    barrier = pltpu.get_barrier_semaphore()
    meet = [dev(z + d, x, yl) for d in (1, 2, 3)] + [dev(z, x + d, yl) for d in (1, 2, 3)]
    meet += [dev(z, x, 1 - yl)] + others
    for d in meet:
        pl.semaphore_signal(barrier, inc=1, device_id=d, device_id_type=MESH)

    @pl.when(z != s)
    def _():
        pl.semaphore_signal(barrier, inc=1, device_id=swapped, device_id_type=MESH)

    pl.semaphore_wait(barrier, jnp.where(z == s, len(meet), len(meet) + 1))

    own, sib = s, yh * 2 + 1 - c
    par, dia = (1 - yh) * 2 + c, (1 - yh) * 2 + 1 - c
    cal, nal = R["call"], R["nall"]
    cot_p = links.copy(cot, cal.at[at256(own), :], partner)
    cot_s = links.copy(cot, cal.at[at256(own), :], sibling)
    cot_p.start()
    cot_s.start()
    cal[at256(own), :] = cot[...]

    gain, shift = vecs[0:1, :], vecs[1:2, :]

    def standard(rows):
        xin = tokens[rows, :].astype(F32)
        cen = xin - jnp.mean(xin, axis=-1, keepdims=True)
        r = lax.rsqrt(jnp.mean(cen * cen, axis=-1, keepdims=True) + 1e-05)
        return xin, cen * r, r

    def norm_strip(u):
        rows = pl.ds(pl.multiple_of(u * 32, 32), 32)
        _, xhat, _ = standard(rows)
        nal[pl.ds(pl.multiple_of(own * 256 + u * 32, 32), 32), :] = (xhat * gain + shift).astype(BF)

    loop(8, norm_strip)
    mine = nal.at[at256(own), :]
    nrm_p = links.copy(mine, mine, partner)
    nrm_s = links.copy(mine, mine, sibling)
    nrm_p.start()
    nrm_s.start()

    sm, smr = R["sm"], R["smr"]
    sm[0] = jnp.zeros((8, 1024), F32)
    sm[0, 1:2, :] = jnp.sum(cot[...].astype(F32), axis=0, keepdims=True)

    start1 = lens[0, 0]
    start2 = start1 + lens[0, 1]
    start3 = start2 + lens[0, 2]

    def doc_of(t):
        return (t >= start1).astype(jnp.int32) + (t >= start2).astype(jnp.int32) + (t >= start3).astype(jnp.int32)

    tab = R["tab"]

    def tables(u):
        rows = pl.ds(pl.multiple_of(u * 64, 64), 64)
        t = lax.broadcasted_iota(jnp.int32, (64, 128), 0) + u * 64
        lane = lax.broadcasted_iota(jnp.int32, (64, 128), 1) % HEAD
        first = jnp.where(t >= start3, start3, jnp.where(t >= start2, start2, jnp.where(t >= start1, start1, 0)))
        offset = (t - first).astype(F32)
        freq = jnp.zeros((64, 128), F32)
        for i in range(ROT // 2):
            freq = jnp.where(lane % (ROT // 2) == i, math.exp(-2.0 * i * math.log(10000.0) / ROT), freq)
        angle = offset * freq
        cosine, sine = jnp.cos(angle), jnp.sin(angle)
        tab[0, rows, :] = jnp.where(lane < ROT, cosine, 1.0)
        tab[1, rows, :] = jnp.where(lane < ROT // 2, -sine, 0.0)
        tab[2, rows, :] = jnp.where((lane >= ROT // 2) & (lane < ROT), sine, 0.0)

    loop(16, tables)

    def rotate(val, rows, sign):
        parts = []
        for p in range(2):
            a = val[:, p * 128 : (p + 1) * 128]
            up = pltpu.roll(a, 128 - ROT // 2, 1) * tab[1, rows, :]
            down = pltpu.roll(a, ROT // 2, 1) * tab[2, rows, :]
            parts.append(a * tab[0, rows, :] + sign * (up + down))
        return jnp.concatenate(parts, axis=1)

    for c_ in loads:
        c_.wait()

    win, wdn, wqkv, wout = R["win"], R["wdn"], R["wqkv"], R["wout"]
    act, gh, hid, ga, outp, gnp = (R[n] for n in ("act", "gh", "hid", "ga", "outp", "gnp"))

    def block(blk):
        rows = at256(blk)
        for j, name in enumerate(("q", "k", "v")):
            b = vecs[4 + j : 5 + j, at256(s)]
            y = dot_nn(nal[rows, :], wqkv[:, j * 256 : (j + 1) * 256]) + b
            if j < 2:
                y = rotate(y, rows, 1.0)
            y = y.astype(BF)
            R[name][rows, :] = y * jnp.asarray(0.125, BF) if j == 0 else y
        R["do"][rows, :] = dot_nt(cal[rows, :], wout[...]).astype(BF)

        def tile(t):
            cs = at256(t)
            hid[...] = dot_nn(nal[rows, :], win[:, cs]) + vecs[pl.ds(7 + s, 1), cs]
            ga[...] = dot_nt(cal[rows, :], wdn[cs, :])

            def strip(u, total):
                r = pl.ds(pl.multiple_of(u * 32, 32), 32)
                h = hid[r, :]
                cdf = 0.5 + 0.5 * lax.erf(h * (1.0 / math.sqrt(2.0)))
                dens = jnp.exp(-0.5 * h * h) * (1.0 / math.sqrt(2.0 * math.pi))
                to = pl.ds(pl.multiple_of(blk * 256 + u * 32, 32), 32)
                act[to, cs] = (h * cdf).astype(BF)
                g = (ga[r, :] * (cdf + h * dens)).astype(BF)
                gh[to, cs] = g
                return total + jnp.sum(g.astype(F32), axis=0, keepdims=True)

            sm[0, 0:1, cs] += lax.fori_loop(0, 8, strip, jnp.zeros((1, 256), F32))

        loop(4, tile)

        def out_tile(n):
            cs = at256(n)
            outp[rows, cs] = dot_nn(act[rows, :], wdn[:, cs])
            gnp[rows, cs] = dot_nt(gh[rows, :], win[cs, :])

        loop(4, out_tile)

    block(own)
    cot_s.wait_recv()
    nrm_s.wait_recv()
    block(sib)
    theirs = cal.at[at256(par), :]
    cot_p.wait_recv()
    cot_f = links.copy(theirs, theirs, sibling)
    cot_f.start()
    theirs = nal.at[at256(par), :]
    nrm_p.wait_recv()
    nrm_f = links.copy(theirs, theirs, sibling)
    nrm_f.start()
    block(par)
    cot_f.wait_recv()
    nrm_f.wait_recv()
    block(dia)
    for c_ in (cot_s, nrm_s, cot_p, nrm_p, cot_f, nrm_f):
        c_.wait_send()

    g_ffn = R["g_ffn"]

    def ffn_grads(m):
        cs = at256(m)
        res = dot_tn(nal[:, cs], gh[...]).astype(BF)
        g_ffn[0, :, :, m] = res.reshape(4, 2, 32, 1024)
        res = dot_tn(act[:, cs], cal[...]).astype(BF)
        g_ffn[1, m] = res.reshape(2, 4, 32, 1024)

    loop(4, ffn_grads)
    ffn = Reduce(links, g_ffn, 1, R["r1_ffn"], R["r2_ffn"], R["ry_ffn"], where)
    ffn_steps = ffn.steps()
    ffn_steps[0]()

    q, k, v, do = R["q"], R["k"], R["v"], R["do"]
    sc, dp, bias, pb, ds = (R[n] for n in ("sc", "dp", "bias", "pb", "ds"))
    dk, dv, dq, mx, mixed, gp = (R[n] for n in ("dk", "dv", "dq", "mx", "mixed", "gp"))
    rxs, rxp = R["rxs"], R["rxp"]
    dk[...] = jnp.zeros((ROW, BLK), F32)
    dv[...] = jnp.zeros((ROW, BLK), F32)
    to_sib = {}
    to_par = {}

    def attend(i):
        n = 256 * (i + 1)
        rows = pl.ds(256 * i, 256)
        keys = pl.ds(0, n)

        def mask(u):
            r = pl.ds(pl.multiple_of(u * 32, 32), 32)
            tr = lax.broadcasted_iota(jnp.int32, (32, n), 0) + (256 * i + u * 32)
            tc = lax.broadcasted_iota(jnp.int32, (32, n), 1)
            ok = (doc_of(tr) == doc_of(tc)) & (tc <= tr)
            bias[r, keys] = jnp.where(ok, 0.0, -1e30)

        loop(8, mask)
        dq[...] = jnp.zeros((BLK, BLK), F32)
        mx[...] = jnp.zeros((BLK, BLK), F32)

        def head(h):
            lanes = lax.broadcasted_iota(jnp.int32, (BLK, BLK), 1) // HEAD == h
            qh = jnp.where(lanes, q[rows, :], jnp.zeros((), BF))
            doh = jnp.where(lanes, do[rows, :], jnp.zeros((), BF))
            sc[:, keys] = dot_nt(qh, k[keys, :])
            dp[:, keys] = dot_nt(doh, v[keys, :])

            def strip(u):
                r = pl.ds(pl.multiple_of(u * 16, 16), 16)
                a = sc[r, keys] + bias[r, keys]
                e = jnp.exp(a - jnp.max(a, axis=-1, keepdims=True))
                p = e * (1.0 / jnp.sum(e, axis=-1, keepdims=True))
                pb[r, keys] = p.astype(BF)
                g = dp[r, keys]
                inner = jnp.sum(p * g, axis=-1, keepdims=True)
                ds[r, keys] = (p * (g - inner)).astype(BF)

            loop(16, strip)
            mx[...] += jnp.where(lanes, dot_nn(pb[:, keys], v[keys, :]), 0.0)
            dq[...] += jnp.where(lanes, dot_nn(ds[:, keys], k[keys, :]), 0.0)
            dk[keys, :] += dot_tn(ds[:, keys], qh)
            dv[keys, :] += dot_tn(pb[:, keys], doh)

        loop(4, head)
        mixed[rows, :] = mx[...].astype(BF)
        grad_q = (dq[...] * 0.125).astype(BF).astype(F32)
        gp[rows, 0:256] = rotate(grad_q, rows, -1.0).astype(BF)
        grad_k = dk[rows, :].astype(BF).astype(F32)
        gp[rows, 256:512] = rotate(grad_k, rows, -1.0).astype(BF)
        gp[rows, 512:768] = dv[rows, :].astype(BF)
        sm[0, 2:3, 0:768] += jnp.sum(gp[rows, :].astype(F32), axis=0, keepdims=True)

        def project(n_):
            cs = at256(n_)
            o = outp[rows, cs] + dot_nn(mixed[rows, :], wout[:, cs])
            outp[rows, cs] = o
            act[rows, cs] = o.astype(BF)
            g = gnp[rows, cs] + dot_nt(gp[rows, :], wqkv[cs, :])
            gnp[rows, cs] = g
            gh[rows, cs] = g.astype(BF)

        loop(4, project)
        j = i // 2
        cps = [links.copy(st.at[rows, :], rxs.at[j, w], sibling) for w, st in enumerate((act, gh))]
        to_sib[i] = cps

        @pl.when(c != i % 2)
        def _():
            for cp in cps:
                cp.start()

    def pass_on(j):
        for i in (2 * j, 2 * j + 1):

            @pl.when(c != i % 2)
            def _(i=i):
                for cp in to_sib[i]:
                    cp.wait_send()

            @pl.when(c == i % 2)
            def _(i=i):
                for cp in to_sib[i]:
                    cp.wait_recv()

        mine_j = at256(2 * j + c)

        @pl.when(yh != j)
        def _():
            def strip(u):
                r = pl.ds(pl.multiple_of((2 * j + c) * 256 + u * 32, 32), 32)
                ru = pl.ds(pl.multiple_of(u * 32, 32), 32)
                act[r, :] = (outp[r, :] + rxs[j, 0, ru, :].astype(F32)).astype(BF)
                gh[r, :] = (gnp[r, :] + rxs[j, 1, ru, :].astype(F32)).astype(BF)

            loop(8, strip)
            for cp in to_par[j]:
                cp.start()

    for j in (0, 1):
        to_par[j] = [links.copy(st.at[at256(2 * j + c), :], rxp.at[w], partner) for w, st in enumerate((act, gh))]

    attend(3)
    ffn_steps[1]()
    attend(2)
    pass_on(1)
    ffn_steps[2]()
    attend(1)
    ffn_steps[3]()
    attend(0)
    pass_on(0)
    ffn_steps[4]()

    g_qkv, g_out = R["g_qkv"], R["g_out"]

    def qkv_grads(m):
        res = dot_tn(nal[:, at256(m)], gp[...]).astype(BF)
        g_qkv[:, :, m] = res.reshape(4, 2, 32, 768)

    loop(4, qkv_grads)
    g_out[...] = dot_tn(mixed[...], cal[...]).reshape(4, 2, 4, 8, 1024)
    att = [
        Reduce(links, g_qkv, 0, R["r1_qkv"], R["r2_qkv"], R["ry_qkv"], where),
        Reduce(links, g_out, 0, R["r1_out"], R["r2_out"], R["ry_out"], where),
    ]
    att_steps = [r.steps() for r in att]

    def att_step(n):
        for st in att_steps:
            st[n]()

    att_step(0)
    ffn_steps[5]()
    finals = []
    fin_in, fin_dn, fin_qkv, fin_out = (R[n] for n in ("fin_in", "fin_dn", "fin_qkv", "fin_out"))
    mine8 = pl.ds(pl.multiple_of(s * 8, 8), 8)

    def spread(src, dst, lane):
        for d in (1, 2, 3):
            t = (s + d) % 4
            cp = links.copy(src.at[pl.ds(pl.multiple_of(t * 8, 8), 8), lane[0]], dst.at[:, lane[1]], (dpi, t))
            cp.start()
            finals.append(cp)
        dst[:, lane[1]] = src[mine8, lane[0]]

    swaps = []

    def swap(src, dst):
        cp = links.copy(src, dst, swapped)
        swaps.append(cp)

        @pl.when(z != s)
        def _():
            cp.start()

        @pl.when(z == s)
        def _():
            dst[...] = src[...]

    fin_in[...] = ffn.own[0].astype(F32) + ffn.land_y[0].astype(F32)
    fin_dn[...] = ffn.own[1].astype(F32) + ffn.land_y[1].astype(F32)
    spread(fin_in, o_win, (slice(None), wide))
    swap(fin_dn, o_wdn)
    att_step(1)

    for cp0, cp1 in zip(to_par[0], to_par[1]):

        @pl.when(yh == 0)
        def _(cp=cp0, cq=cp1):
            cp.wait_recv()
            cq.wait_send()

        @pl.when(yh == 1)
        def _(cp=cp1, cq=cp0):
            cp.wait_recv()
            cq.wait_send()

    def last_strip(u, carry):
        sg, sb = carry
        ru = pl.ds(pl.multiple_of(u * 16, 16), 16)
        r = pl.ds(pl.multiple_of(own * 256 + u * 16, 16), 16)
        xin, xhat, rs = standard(ru)
        total = outp[r, :] + rxs[yh, 0, ru, :].astype(F32) + rxp[0, ru, :].astype(F32)
        o_out[ru, :] = (xin + total + vecs[2:3, :] + vecs[3:4, :]).astype(BF)
        gn = gnp[r, :] + rxs[yh, 1, ru, :].astype(F32) + rxp[1, ru, :].astype(F32)
        n = gn * gain
        back = rs * (n - jnp.mean(n, axis=-1, keepdims=True) - xhat * jnp.mean(n * xhat, axis=-1, keepdims=True))
        o_tok[ru, :] = cot[ru, :].astype(F32) + back
        sg = sg + jnp.sum(gn * xhat, axis=0, keepdims=True)
        sb = sb + jnp.sum(gn, axis=0, keepdims=True)
        return sg, sb

    zero = jnp.zeros((1, D), F32)
    sg, sb = lax.fori_loop(0, 16, last_strip, (zero, zero))
    sm[0, 3:4, :] = sg
    sm[0, 4:5, :] = sb

    def exchange(level, slot, devices):
        cps = [links.copy(sm.at[level], smr.at[slot + d], t) for d, t in enumerate(devices)]
        for cp in cps:
            cp.start()
        return cps

    def gather(level, slot, cps):
        for cp in cps:
            cp.wait()
        total = sm[level]
        for d in range(len(cps)):
            total = total + smr[slot + d]
        sm[level + 1] = total

    cps = exchange(0, 0, [dev(z + d, x, yl) for d in (1, 2, 3)])
    att_step(2)
    gather(0, 0, cps)
    cps = exchange(1, 3, [dev(z, x + d, yl) for d in (1, 2, 3)])
    att_step(3)
    gather(1, 3, cps)
    cps = exchange(2, 6, [dev(z, x, 1 - yl)])
    att_step(4)
    gather(2, 6, cps)
    cps = exchange(3, 7, others)
    att_step(5)
    fin_qkv[...] = att[0].own[...].astype(F32) + att[0].land_y[...].astype(F32)
    fin_out[...] = att[1].own[...] + att[1].land_y[...]
    for j in range(3):
        spread(fin_qkv, o_wqkv, (pl.ds(j * 256, 256), pl.ds(pl.multiple_of(j * 1024 + s * 256, 256), 256)))
    swap(fin_out, o_wout)
    for cp in cps:
        cp.wait()
    o_small[s] = sm[3]
    for d in range(3):
        o_small[(s + 3 - d) % 4] = smr[7 + d]
    for cp in finals:
        cp.wait()

    @pl.when(z != s)
    def _():
        for cp in swaps:
            cp.wait()

    assert links.count <= NSEM, links.count


def on_device(tokens, lengths, ln_gain, ln_bias, w_qkv, b_qkv, w_out, b_out, w_in, b_in, w_down, b_down, cotangent):
    vecs = jnp.concatenate([ln_gain, ln_bias, b_out, b_down, b_qkv, b_in, jnp.zeros((5 * D,), BF)])
    vecs = vecs.reshape(16, D).astype(F32)
    V = pl.BlockSpec(memory_space=pltpu.VMEM)
    H = pl.BlockSpec(memory_space=pl.ANY)
    S = pl.BlockSpec(memory_space=pltpu.SMEM)
    sds = jax.ShapeDtypeStruct
    outs = pl.pallas_call(
        kernel,
        out_shape=[
            sds((BLK, D), BF),
            sds((BLK, D), F32),
            sds((8, 3 * D), F32),
            sds((8, D), F32),
            sds((8, 4 * D), F32),
            sds((32, D), F32),
            sds((4, 8, 1024), F32),
        ],
        in_specs=[V, S, V, V, H, H, H, H],
        out_specs=[V] * 7,
        scratch_shapes=[pltpu.VMEM(shape, dt) for _, shape, dt in SCRATCH]
        + [pltpu.SemaphoreType.DMA((NSEM,)), pltpu.SemaphoreType.DMA((NSEM,)), pltpu.SemaphoreType.DMA((NLOC,))],
        compiler_params=pltpu.CompilerParams(collective_id=0, has_side_effects=True, vmem_limit_bytes=VMEM_LIMIT),
        name="layer",
    )(vecs, lengths, tokens[0], cotangent[0], w_qkv, w_out, w_in, w_down)
    out, grad_tokens, g_wqkv, g_wout, g_win, g_wdn, small = outs
    index = lax.axis_index("dp") * 4 + lax.axis_index("seq")

    def share(vec):
        n = vec.shape[0] // 128
        return lax.dynamic_slice_in_dim(vec, index * n, n)

    g_bin = share(small[:, 0].reshape(4096))
    g_bout = share(jnp.sum(small[:, 1], axis=0))
    g_bqkv = share(small[:, 2, :768].reshape(4, 3, 256).transpose(1, 0, 2).reshape(3072))
    g_gain = share(jnp.sum(small[:, 3], axis=0))
    g_bias = share(jnp.sum(small[:, 4], axis=0))
    return (out[None], grad_tokens[None], g_gain, g_bias, g_wqkv, g_bqkv, g_wout, g_bout, g_win, g_bin, g_wdn, g_bout)


def solution(mesh):
    act, vec, mat = P("dp", "seq", None), P(("dp", "seq")), P(("dp", "seq"), None)
    return jax.shard_map(
        on_device,
        mesh=mesh,
        in_specs=(act, P("dp", None)) + (P(),) * 10 + (act,),
        out_specs=(act, act, vec, vec, mat, vec, mat, vec, mat, vec, mat, vec),
        check_vma=False,
    )
```

time: 2780 us -> 219 us (0.08)
  waiting for transfers between devices: 2400 us -> 0 us
  Pallas kernels: 0 us -> 197 us
  matrix products: 141 us -> 0 us
  blocking collectives: 82.7 us -> 0 us
  local copies, waits for them, and re-layouts: 57.4 us -> 18.9 us
  starting transfers between devices: 34.3 us -> 0 us
  other arithmetic: 30.7 us -> 1.21 us
    reduce_scatter x4 -> x0, waiting for transfers between devices: 2360 us -> none  [the longest x1 666 us: on_device(): lax.psum_scatter(grad_w_down, ('dp', 'seq'), scatter_dimension=0, tiled=T...]
    pallas_call x0 -> x1, Pallas kernels: none -> 197 us  [on_device(): pl.pallas_call(kernel, out_shape=[sds((BLK, D), BF), sds((BLK, D), F32),...]
    dot_general x26 -> x0, matrix products: 141 us -> none  [the longest x4 29.7 us: contract_rows(): lax.dot_general(left, right, (((0,), (0,)), ((), ())), preferred_element_...]
    unnamed x1 -> x0, blocking collectives: 67.5 us -> none
    all_to_all x7 -> x0, starting transfers between devices: 33.9 us -> none  [the longest x1 5.39 us: on_device(): lax.all_to_all(grad_query_h, 'seq', split_axis=0, concat_axis=1, tiled=True)]
    all_to_all x7 -> x0, waiting for transfers between devices: 32.9 us -> none  [the longest x1 7.85 us: on_device(): lax.all_to_all(grad_value_h, 'seq', split_axis=0, concat_axis=1, tiled=True)]
  transfers between devices with their start and end apart: 11 -> 0, of which waited for: 10 -> 0; matrix products, arithmetic and copies ran while one was open for 7% -> 0% of each run, Pallas kernels for 0% -> 0%
where the time goes in v1:
time: 219 us; the launch traced here: 218 us
  Pallas kernels  197 us (90%)
  local copies, waits for them, and re-layouts  18.9 us (9%)
    pallas_call x1, Pallas kernels, on_device(): pl.pallas_call(kernel, out_shape=[sds((BLK, D), BF), sds((BLK, D), F32),...  197 us
    unnamed x16, local copies, waits for them, and re-layouts  14.9 us

profile of v1, /device:TPU:1, one launch (start us, length us, event | category | flops | bytes accessed | tf_op | source)
XLA Modules:
  0.0 218.3 jit_solution(17317254140069569099)
XLA Ops:
  0.7 0.7 constant_dynamic-update-slice_fusion.5
  1.3 0.7 constant_dynamic-update-slice_fusion.4
  2.0 0.7 constant_dynamic-update-slice_fusion.3
  2.7 0.7 constant_dynamic-update-slice_fusion.2
  3.4 0.7 constant_dynamic-update-slice_fusion.1
  4.1 0.7 constant_dynamic-update-slice_fusion
  4.8 0.6 reshape.31.refs_0_
  5.5 197.5 %layer.1 = (bf16[256,1024]{1,0:T(8,128)(2,1)}, f32[256,1024]{1,0:T(8,128)}, f32[8,3072]{1,0:T(8,128)}, f32[8,1024]{1,0:T(8,128)}, f32[8,4096]{1,0:T(8,128)}, /*index=5*/f32[32,1024]{1,0:T(8,128)}, f32[4,8,1024]{2,1,0:T(8,128)}) custom-call(f32[16,1024]{1,0:T(8,128)} %reshape.31.refs_0_, s32[1,4]{1,0:T(1,128)} %refs_1_.1, bf16[256,1024]{1,0:T(8,128)(2,1)} %bitcast.11, ...), custom_call_target="tpu_custom_call" | custom-call | tf_op jit(solution)/shard_map/layer/pallas_call | solution.py:645
  203.0 1.2 slice_reduce_fusion
  204.2 0.1 dynamic_slice.18
  204.2 0.0 copy-start
  204.2 0.6 dynamic_slice.15
  204.8 0.6 dynamic_slice.16
  205.4 0.6 dynamic_slice.19
  206.0 0.9 slice.17
  206.9 0.6 dynamic_slice.17
  207.5 0.5 copy.40
  208.0 1.9 copy.41
  209.9 2.3 %copy.42 = f32[1,256,1024]{2,1,0:T(8,128)} copy(f32[1,256,1024]{2,1,0:T(8,128)} %bitcast.10) | data formatting | bytes 2097152
  212.2 1.5 copy.43
  213.7 1.4 copy.44
  215.1 1.6 copy.45
  216.7 1.6 copy.46
  218.3 0.0 copy-done
  (3 shorter events, 0.0 us)
Async XLA Ops:
  204.2 14.0 %copy-start = (f32[8]{0:T(128)}, f32[8]{0:T(128)S(1)}, u32[]{:S(2)}) copy-start(f32[8]{0:T(128)S(1)} %dynamic_slice.18) | copy-start | bytes 100

commit v2 on v1

v2 whole, which is shorter than its diff:
```python
import math

import jax
import jax.numpy as jnp
from jax import lax
from jax.experimental import pallas as pl
from jax.experimental.pallas import tpu as pltpu
from jax.sharding import PartitionSpec as P

HEAD = 64
ROT = 16
ROW = 1024
D = 1024
BLK = 256
BF = jnp.bfloat16
F32 = jnp.float32
MESH = pl.DeviceIdType.MESH
VMEM_LIMIT = 63 * 2**20


def dot_nn(a, b):
    return lax.dot_general(a, b, (((1,), (0,)), ((), ())), preferred_element_type=F32)


def dot_nt(a, b):
    return lax.dot_general(a, b, (((1,), (1,)), ((), ())), preferred_element_type=F32)


def dot_tn(a, b):
    return lax.dot_general(a, b, (((0,), (0,)), ((), ())), preferred_element_type=F32)


def loop(count, step):
    def run(i, carry):
        step(i)
        return carry

    lax.fori_loop(0, count, run, 0)


def at256(i):
    return pl.ds(pl.multiple_of(i * 256, 256), 256)


SCRATCH = [
    ("vecs", (16, D), F32),
    ("win", (2, D, 1024), BF),
    ("wdn", (2, 1024, D), BF),
    ("wqkv", (2, 2, D, 384), BF),
    ("wout", (2, BLK, D), BF),
    ("nall", (ROW, D), BF),
    ("call", (ROW, D), BF),
    ("q", (2, ROW, 128), BF),
    ("k", (2, ROW, 128), BF),
    ("v", (2, ROW, 128), BF),
    ("do", (2, ROW, 128), BF),
    ("kt", (2, 128, ROW), BF),
    ("vt", (2, 128, ROW), BF),
    ("qh", (2, BLK, 128), BF),
    ("doh", (2, BLK, 128), BF),
    ("act", (ROW, 1024), BF),
    ("gh", (ROW, 1024), BF),
    ("g_ffn", (2, 2, 4, 4, 4, 16, 1024), BF),
    ("g_qkv", (2, 4, 2, 4, 32, 384), BF),
    ("g_out", (4, 2, 4, 16, 512), BF),
    ("outp", (512, D), F32),
    ("gnp", (512, D), F32),
    ("sc", (2, ROW, BLK), F32),
    ("dp", (2, ROW, BLK), F32),
    ("bias", (ROW, BLK), F32),
    ("dk", (ROW, 128), F32),
    ("dv", (ROW, 128), F32),
    ("dq", (128, BLK), F32),
    ("mx", (128, BLK), F32),
    ("xr", (512, 1024), BF),
    ("tab", (2, ROW, 128), F32),
    ("mr", (2, BLK, 128), F32),
    ("sm", (4, 8, 1024), F32),
    ("smr", (10, 8, 1024), F32),
    ("rxs", (2, BLK, D), BF),
    ("r1z_ffn", (2, 6, 2, 4, 2, 16, 512), BF),
    ("r1x_ffn", (2, 6, 2, 2, 4, 16, 512), BF),
    ("r2_ffn", (2, 2, 6, 2, 2, 16, 512), BF),
    ("r3_ffn", (2, 3, 2, 16, 1024), BF),
    ("r1z_qkv", (2, 6, 4, 32, 256), BF),
    ("r1x_qkv", (2, 6, 4, 32, 256), BF),
    ("r2_qkv", (2, 2, 6, 32, 256), BF),
    ("r3_qkv", (2, 1, 32, 384), BF),
    ("r1z_out", (6, 4, 16, 256), BF),
    ("r1x_out", (6, 4, 16, 256), BF),
    ("r2_out", (2, 6, 16, 256), BF),
    ("r3_out", (1, 16, 512), BF),
    ("fin_ffn", (2, 2, 16, 1024), F32),
    ("fin_qkv", (2, 32, 384), F32),
    ("fin_out", (16, 512), F32),
]
CH = 256
NSEM = 200
NLOC = 20


class Links:
    def __init__(self, send, recv):
        self.send, self.recv, self.count = send, recv, 0

    def copy(self, src, dst, device):
        k = self.count
        self.count += 1
        return pltpu.make_async_remote_copy(
            src_ref=src,
            dst_ref=dst,
            send_sem=self.send.at[k],
            recv_sem=self.recv.at[k],
            device_id=device,
            device_id_type=MESH,
        )


def add_into(dst, sources):
    if len(dst.shape) > 2:
        for i in range(dst.shape[0]):
            add_into(dst.at[i], [s.at[i] for s in sources])
        return
    total = dst[...].astype(F32)
    for s in sources:
        total = total + s[...].astype(F32)
    dst[...] = total.astype(dst.dtype)


class Ring:
    def __init__(self, links, block, pos, right, left, land):
        self.block, self.land = block, land
        self.pos = pos
        self.rt, self.lf, self.opp = (pos + 1) % 4, (pos + 3) % 4, (pos + 2) % 4
        c = links.copy
        self.early = [
            c(block(self.opp, 0), land.at[0], right),
            c(block(self.opp, 1), land.at[1], left),
            c(block(self.rt, 1), land.at[2], right),
            c(block(self.lf, 0), land.at[3], left),
        ]
        self.late = [
            c(block(self.rt, 0), land.at[4], right),
            c(block(self.lf, 1), land.at[5], left),
        ]

    def start(self):
        for c in self.early:
            c.start()

    def middle(self):
        self.early[0].wait_recv()
        add_into(self.block(self.rt, 0), [self.land.at[0]])
        self.late[0].start()
        self.early[1].wait_recv()
        add_into(self.block(self.lf, 1), [self.land.at[1]])
        self.late[1].start()

    def finish(self):
        for c in self.early[2:] + self.late:
            c.wait_recv()
        add_into(self.block(self.pos, 0), [self.land.at[4], self.land.at[3]])
        add_into(self.block(self.pos, 1), [self.land.at[2], self.land.at[5]])
        for c in self.early + self.late:
            c.wait_send()


class Reduce:
    def __init__(self, links, ref, lead, lands, pos, at_z, at_x, last, after, half):
        z, x, y = pos
        pre = (slice(None),) * lead
        every = slice(None)
        first, second = pl.ds(0, half), pl.ds(half, ref.shape[-1] - half)
        ny = ref.shape[lead + 1] // 2
        land1z, land1x, land2z, land2x, self.land_y = lands

        def view(a, h, b, cols):
            hh = h if ny == 1 else pl.ds(h * ny, ny)
            return ref.at[pre + (a, hh, b, every, cols)]

        zr, zl, xr, xl = at_z(1), at_z(3), at_x(1), at_x(3)
        self.one = [
            Ring(links, lambda t, h: view(every, h, t, first), z, zr, zl, land1z),
            Ring(links, lambda t, h: view(t, h, every, second), x, xr, xl, land1x),
        ]
        self.two = [
            Ring(links, lambda t, h: view(t, h, z, first), x, xr, xl, land2z),
            Ring(links, lambda t, h: view(x, h, t, second), z, zr, zl, land2x),
        ]
        self.own = ref.at[pre + (x, y, z)]
        self.last = [links.copy(ref.at[pre + (x, ty, z)], self.land_y.at[n], d) for n, (ty, d) in enumerate(last)]
        self.after = after
        self.at = 0

    def result(self, index=()):
        total = self.own[index or ...].astype(F32)
        for n in range(len(self.last)):
            total = total + self.land_y[(n,) + index].astype(F32)
        return total

    def step(self):
        one, two = self.one, self.two
        if self.at == 0:
            for r in one:
                r.start()
        elif self.at == 1:
            for r in one:
                r.middle()
        elif self.at == 2:
            for r, n in zip(one, two):
                r.finish()
            for n in two:
                n.start()
        elif self.at == 3:
            for r in two:
                r.middle()
        elif self.at == 4:
            for r in two:
                r.finish()
            for cp in self.last:
                cp.start()
        elif self.at == 5:
            for cp in self.last:
                cp.wait()
            self.after(self)
        self.at += 1


def kernel(*refs):
    small, (lens, tokens, cot, w_qkv, w_out, w_in, w_down) = refs[:6], refs[6:13]
    (o_out, o_tok, o_wqkv, o_wout, o_win, o_wdn, o_small) = refs[13:20]
    rest = refs[20:]
    R = {name: r for (name, _, _), r in zip(SCRATCH, rest)}
    send, recv, loc = rest[len(SCRATCH) :]
    links = Links(send, recv)

    dpi, s = lax.axis_index("dp"), lax.axis_index("seq")
    z, x, yl = dpi // 8, (dpi // 2) % 4, dpi % 2
    yh, c = s // 2, s % 2
    y = yh * 2 + yl

    def dev(zz, xx, yy, cc):
        return ((zz % 4) * 8 + (xx % 4) * 2 + (yy % 4) % 2, ((yy % 4) // 2) * 2 + cc)

    def at_z(d):
        return dev(z + d, x, y, c)

    def at_x(d):
        return dev(z, x + d, y, c)

    def at_y(d):
        return dev(z, x, y + d, c)

    sibling = dev(z, x, y, 1 - c)
    partner = dev(z, x, y + 2, c)
    diagonal = dev(z, x, y + 2, 1 - c)

    loads = []

    def load(src, dst):
        cp = pltpu.make_async_copy(src, dst, loc.at[len(loads)])
        cp.start()
        loads.append(cp)

    for a in range(2):
        wide = pl.ds(pl.multiple_of((2 * a + c) * 1024, 1024), 1024)
        load(w_in.at[:, wide], R["win"].at[a])
        load(w_down.at[wide, :], R["wdn"].at[a])
    for w, sw in enumerate((s, (1 - yh) * 2 + c)):
        load(w_out.at[at256(sw), :], R["wout"].at[w])
        for g in range(2):
            for j in range(3):
                cols = pl.ds(pl.multiple_of(j * 1024 + sw * 256 + g * 128, 128), 128)
                load(w_qkv.at[:, cols], R["wqkv"].at[w, g, :, pl.ds(j * 128, 128)])

    meet = [at_x(d) for d in (1, 2, 3)] + [at_y(d) for d in (1, 2, 3)] + [sibling, diagonal]
    for d in (1, 2, 3):
        for cc in (c, 1 - c):
            meet += [dev(z + d, x, y, cc), dev(z + d, x, y + 2, cc)]
    barrier = pltpu.get_barrier_semaphore()
    for d in meet:
        pl.semaphore_signal(barrier, inc=1, device_id=d, device_id_type=MESH)
    pl.semaphore_wait(barrier, len(meet))

    own, sib = s, yh * 2 + 1 - c
    par, dia = (1 - yh) * 2 + c, (1 - yh) * 2 + 1 - c
    cal, nal = R["call"], R["nall"]
    cot_s = links.copy(cot, cal.at[at256(own), :], sibling)
    cot_p = links.copy(cot, cal.at[at256(own), :], partner)
    cot_s.start()
    cot_p.start()
    cal[at256(own), :] = cot[...]

    vecs, row = R["vecs"], 0
    for ref in small:
        for i in range(ref.shape[0] // D):
            vecs[row : row + 1, :] = ref[pl.ds(i * D, D)].astype(F32).reshape(1, D)
            row += 1
    gain, shift = vecs[0:1, :], vecs[1:2, :]
    mr = R["mr"]

    def norm_strip(u, carry):
        rows = pl.ds(pl.multiple_of(u * 32, 32), 32)
        xin = tokens[rows, :].astype(F32)
        mean = jnp.mean(xin, axis=-1, keepdims=True)
        cen = xin - mean
        r = lax.rsqrt(jnp.mean(cen * cen, axis=-1, keepdims=True) + 1e-05)
        mr[0, rows, :] = jnp.broadcast_to(mean, (32, 128))
        mr[1, rows, :] = jnp.broadcast_to(r, (32, 128))
        nal[pl.ds(pl.multiple_of(own * 256 + u * 32, 32), 32), :] = (cen * r * gain + shift).astype(BF)
        return carry

    lax.fori_loop(0, 8, norm_strip, 0, unroll=2)
    mine = nal.at[at256(own), :]
    nrm_s = links.copy(mine, mine, sibling)
    nrm_p = links.copy(mine, mine, partner)
    nrm_s.start()
    nrm_p.start()

    sm, smr = R["sm"], R["smr"]
    sm[0] = jnp.zeros((8, 1024), F32)
    sm[0, 4:5, :] = jnp.sum(cot[...].astype(F32), axis=0, keepdims=True)

    start1 = lens[0, 0]
    start2 = start1 + lens[0, 1]
    start3 = start2 + lens[0, 2]

    def first_of(t):
        return jnp.where(t >= start3, start3, jnp.where(t >= start2, start2, jnp.where(t >= start1, start1, 0)))

    tab = R["tab"]

    def tables(u):
        rows = pl.ds(pl.multiple_of(u * 64, 64), 64)
        t = lax.broadcasted_iota(jnp.int32, (64, 128), 0) + u * 64
        lane = lax.broadcasted_iota(jnp.int32, (64, 128), 1) % HEAD
        offset = (t - first_of(t)).astype(F32)
        freq = jnp.zeros((64, 128), F32)
        for i in range(ROT // 2):
            freq = jnp.where(lane % (ROT // 2) == i, math.exp(-2.0 * i * math.log(10000.0) / ROT), freq)
        angle = offset * freq
        cosine, sine = jnp.cos(angle), jnp.sin(angle)
        tab[0, rows, :] = jnp.where(lane < ROT, cosine, 1.0)
        tab[1, rows, :] = jnp.where(lane < ROT // 2, -sine, jnp.where(lane < ROT, sine, 0.0))

    loop(16, tables)
    low_lane = lax.broadcasted_iota(jnp.int32, (BLK, 128), 1) % HEAD < ROT // 2

    def rotate(val, rows, sign):
        other = jnp.where(low_lane, pltpu.roll(val, 128 - ROT // 2, 1), pltpu.roll(val, ROT // 2, 1))
        return val * tab[0, rows, :] + sign * other * tab[1, rows, :]

    for cp in loads:
        cp.wait()

    win, wdn, wqkv, wout = R["win"], R["wdn"], R["wqkv"], R["wout"]
    act, gh, outp, gnp = (R[n] for n in ("act", "gh", "outp", "gnp"))
    hid, ga = R["sc"].at[0, pl.ds(0, 512)], R["dp"].at[0, pl.ds(0, 512)]
    q, k, v, do, kt, vt, qh, doh = (R[n] for n in ("q", "k", "v", "do", "kt", "vt", "qh", "doh"))

    def qkv_block(blk):
        rows = at256(blk)
        for g in range(2):
            yv = dot_nn(nal[rows, :], wqkv[0, g])
            for j, dst in enumerate((q, k, v)):
                b = vecs[4 + j : 5 + j, pl.ds(pl.multiple_of(s * 256 + g * 128, 128), 128)]
                part = yv[:, j * 128 : (j + 1) * 128] + b
                if j < 2:
                    part = rotate(part, rows, 1.0)
                part = part.astype(BF)
                dst[g, rows, :] = part * jnp.asarray(0.125, BF) if j == 0 else part
                if j > 0:
                    (kt, vt)[j - 1][g, :, rows] = jnp.transpose(part)
        d = dot_nt(cal[rows, :], wout[0]).astype(BF)
        do[0, rows, :] = d[:, 0:128]
        do[1, rows, :] = d[:, 128:256]

    here = pl.ds(pl.multiple_of(yh * 512, 512), 512)
    there = pl.ds(pl.multiple_of((1 - yh) * 512, 512), 512)

    def ffn_tiles(a):
        half = pl.ds(a * 512, 512)

        def tile(t):
            cs = at256(t)
            hid[...] = dot_nn(nal[here, :], win[a, :, cs]) + vecs[pl.ds(7 + 2 * a + c, 1), cs]
            ga[...] = dot_nt(cal[here, :], wdn[a, cs, :])

            def strip(u, total):
                r = pl.ds(pl.multiple_of(u * 32, 32), 32)
                h = hid[r, :]
                cdf = 0.5 + 0.5 * lax.erf(h * (1.0 / math.sqrt(2.0)))
                dens = jnp.exp(-0.5 * h * h) * (1.0 / math.sqrt(2.0 * math.pi))
                to = pl.ds(pl.multiple_of(a * 512 + u * 32, 32), 32)
                act[to, cs] = (h * cdf).astype(BF)
                grad = (ga[r, :] * (cdf + h * dens)).astype(BF)
                gh[to, cs] = grad
                return total + jnp.sum(grad.astype(F32).reshape(4, 8, 256), axis=0)

            total = lax.fori_loop(0, 16, strip, jnp.zeros((8, 256), F32), unroll=2)
            sm[0, a : a + 1, cs] = jnp.sum(total, axis=0, keepdims=True)

        loop(4, tile)

    g_ffn = R["g_ffn"]

    def ffn_grads(a):
        half = pl.ds(a * 512, 512)

        def part(m):
            cs = at256(m)
            res = dot_tn(nal[here, cs], gh[half, :]).astype(BF)
            g_ffn[a, 0, :, :, m] = res.reshape(4, 4, 16, 1024)
            res = dot_tn(act[half, cs], cal[here, :]).astype(BF)
            g_ffn[a, 1, m] = res.reshape(4, 4, 16, 1024)

        loop(4, part)

    def ffn_out(n):
        cs = at256(n)
        top, low = pl.ds(0, 512), pl.ds(512, 512)
        outp[:, cs] = dot_nn(act[top, :], wdn[0, :, cs]) + dot_nn(act[low, :], wdn[1, :, cs])
        gnp[:, cs] = dot_nt(gh[top, :], win[0, cs, :]) + dot_nt(gh[low, :], win[1, cs, :])

    finals = []

    def put(src, dst, device, sends=None, arrives=None):
        cp = links.copy(src, dst, device)
        finals.append((cp, sends, arrives))
        if sends is None:
            cp.start()
        else:
            pl.when(sends)(cp.start)

    def keep(src, dst, here_too):
        @pl.when(here_too)
        def _():
            dst[...] = src[...]

    fin_ffn, fin_qkv, fin_out = R["fin_ffn"], R["fin_qkv"], R["fin_out"]

    def ffn_done(a):
        def done(red):
            for w in range(2):
                fin_ffn[a, w] = red.result((w,))
            cols = pl.ds(pl.multiple_of((2 * a + c) * 1024, 1024), 1024)
            theirs = pl.ds(pl.multiple_of((1 - c) * 8, 8), 8)
            put(fin_ffn.at[a, 0, theirs, :], o_win.at[:, cols], sibling)
            o_win[:, cols] = fin_ffn[a, 0, pl.ds(pl.multiple_of(c * 8, 8), 8), :]
            to = dev(2 * a + c, x, y, z // 2)
            for h in range(2):
                rows, right = pl.ds(h * 16, 16), z % 2 == h
                here_too = (z == 2 * a + c) & (z // 2 == c)
                from_here = (z == 2 * c + h) & (z % 2 == c)
                sends = right & jnp.logical_not(here_too)
                arrives = (z // 2 == a) & jnp.logical_not(from_here)
                put(fin_ffn.at[a, 1], o_wdn.at[rows, :], to, sends, arrives)
                keep(fin_ffn.at[a, 1], o_wdn.at[rows, :], right & here_too)

        return done

    def qkv_done(g):
        def done(red):
            fin_qkv[g] = red.result()
            for j in range(3):
                src_l = pl.ds(j * 128, 128)
                dst_l = pl.ds(pl.multiple_of(j * 1024 + s * 256 + g * 128, 128), 128)
                for d in (1, 2, 3):
                    t = (s + d) % 4
                    put(fin_qkv.at[g, pl.ds(pl.multiple_of(t * 8, 8), 8), src_l], o_wqkv.at[:, dst_l], (dpi, t))
                o_wqkv[:, dst_l] = fin_qkv[g, pl.ds(pl.multiple_of(s * 8, 8), 8), src_l]

        return done

    def out_done(red):
        fin_out[...] = red.result()
        for cc in range(2):
            to = dev(s, x, (z // 2) * 2 + yl, cc)
            src = fin_out.at[pl.ds(cc * 8, 8), :]
            for h in range(2):
                dst, right = o_wout.at[:, pl.ds(h * 512, 512)], z % 2 == h
                here_too = (z == s) & (z // 2 == yh) & (c == cc)
                from_here = (z == 2 * yh + h) & (s == z)
                sends = right & jnp.logical_not(here_too)
                arrives = (c == cc) & jnp.logical_not(from_here)
                put(src, dst, to, sends, arrives)
                keep(src, dst, right & here_too)

    def place(yy):
        return (yy % 2) * 2 + (yy % 4) // 2

    def reduce_ffn(a):
        last = [(place(y + d), at_y(d)) for d in (1, 2, 3)]
        lands = (R["r1z_ffn"].at[a], R["r1x_ffn"].at[a], R["r2_ffn"].at[a, 0], R["r2_ffn"].at[a, 1], R["r3_ffn"].at[a])
        return Reduce(links, g_ffn.at[a], 1, lands, (z, x, place(y)), at_z, at_x, last, ffn_done(a), 512)

    last_yl = [(1 - yl, dev(z, x, yh * 2 + 1 - yl, c))]

    def reduce_qkv(g):
        half = 256 if g == 0 else 128
        one, two = pl.ds(0, half), pl.ds(0, 384 - half)
        lands = (R["r1z_qkv"].at[g, :, :, :, one], R["r1x_qkv"].at[g, :, :, :, two])
        lands += (R["r2_qkv"].at[g, 0, :, :, one], R["r2_qkv"].at[g, 1, :, :, two], R["r3_qkv"].at[g])
        return Reduce(links, R["g_qkv"].at[g], 0, lands, (z, x, yl), at_z, at_x, last_yl, qkv_done(g), half)

    def reduce_out():
        lands = (R["r1z_out"], R["r1x_out"], R["r2_out"].at[0], R["r2_out"].at[1], R["r3_out"])
        return Reduce(links, R["g_out"], 0, lands, (z, x, yl), at_z, at_x, last_yl, out_done, 256)

    sc, dp, bias = R["sc"], R["dp"], R["bias"]
    pb = [win.at[0, :, pl.ds(u * 256, 256)] for u in range(2)]
    ds = [win.at[0, :, pl.ds(512 + u * 256, 256)] for u in range(2)]
    dk, dv, dq, mx = (R[n] for n in ("dk", "dv", "dq", "mx"))
    xo, xr = act, R["xr"]
    g_qkv, g_out = R["g_qkv"], R["g_out"]

    def attend(g, i):
        n = 256 * (i + 1)
        rows = pl.ds(256 * i, 256)
        keys = pl.ds(0, n)
        chunks = [pl.ds(j * CH, CH) for j in range(n // CH)]

        def fold(a, op):
            return op(a.reshape(CH // 8, 8, BLK), axis=0)

        def mask(j):
            tk = lax.broadcasted_iota(jnp.int32, (128, BLK), 0) + j * 128
            tq = lax.broadcasted_iota(jnp.int32, (128, BLK), 1) + 256 * i
            ok = (tk >= first_of(tq)) & (tk <= tq)
            bias[pl.ds(pl.multiple_of(j * 128, 128), 128), :] = jnp.where(ok, 0.0, -1e30)

        loop(n // 128, mask)
        heads = range(2)
        tops, stats = [], []
        for u in heads:
            lanes = lax.broadcasted_iota(jnp.int32, (BLK, 128), 1) // HEAD == u
            qh[u] = jnp.where(lanes, q[g, rows, :], jnp.zeros((), BF))
            doh[u] = jnp.where(lanes, do[g, rows, :], jnp.zeros((), BF))
        for u in heads:
            top = jnp.full((8, BLK), -1e30, F32)
            for ch in chunks:
                a = dot_nt(k[g, ch, :], qh[u]) + bias[ch, :]
                sc[u, ch, :] = a
                top = jnp.maximum(top, fold(a, jnp.max))
            tops.append(jnp.max(top, axis=0, keepdims=True))
        for u in heads:
            total, inner = jnp.zeros((8, BLK), F32), jnp.zeros((8, BLK), F32)
            for ch in chunks:
                gr = dot_nt(v[g, ch, :], doh[u])
                dp[u, ch, :] = gr
                e = jnp.exp(sc[u, ch, :] - tops[u])
                sc[u, ch, :] = e
                total, inner = total + fold(e, jnp.sum), inner + fold(e * gr, jnp.sum)
            inv = 1.0 / jnp.sum(total, axis=0, keepdims=True)
            stats.append((inv, jnp.sum(inner, axis=0, keepdims=True) * inv))
        for u in heads:
            inv, inner = stats[u]
            for j, ch in enumerate(chunks):
                p = sc[u, ch, :] * inv
                p_low = p.astype(BF)
                d_low = (p * (dp[u, ch, :] - inner)).astype(BF)
                pb[u][ch, :] = p_low
                ds[u][ch, :] = d_low
                if i == 3 and u == 0:
                    dk[ch, :] = dot_nn(d_low, qh[u])
                    dv[ch, :] = dot_nn(p_low, doh[u])
                else:
                    dk[ch, :] += dot_nn(d_low, qh[u])
                    dv[ch, :] += dot_nn(p_low, doh[u])
        for u in heads:
            hr = pl.ds(u * HEAD, HEAD)
            mx[hr, :] = dot_nn(vt[g, hr, keys], pb[u][keys, :])
            dq[hr, :] = dot_nn(kt[g, hr, keys], ds[u][keys, :])

        def place_in(j, val):
            xo[rows, pl.ds(g * 512 + j * 128, 128)] = val

        place_in(3, jnp.transpose(mx[...]).astype(BF))
        grad_q = jnp.transpose(dq[...] * 0.125).astype(BF).astype(F32)
        place_in(0, rotate(grad_q, rows, -1.0).astype(BF))
        grad_k = dk[rows, :].astype(BF).astype(F32)
        place_in(1, rotate(grad_k, rows, -1.0).astype(BF))
        place_in(2, dv[rows, :].astype(BF))

    back = []

    def send_back(g):
        cols = pl.ds(g * 512, 512)
        cp = links.copy(xo.at[there, cols], xr.at[:, cols], partner)
        cp.start()
        back.append(cp)

    def qkv_grads(g):
        def part(m):
            res = dot_tn(nal[:, at256(m)], xo[:, pl.ds(g * 512, 384)]).astype(BF)
            g_qkv[g, :, :, m] = res.reshape(4, 2, 32, 384)

        loop(4, part)

    def bias_grads(g):
        total = jnp.zeros((8, 384), F32)

        def part(u, total):
            r = pl.ds(pl.multiple_of(u * 64, 64), 64)
            return total + jnp.sum(xo[r, pl.ds(g * 512, 384)].astype(F32).reshape(8, 8, 384), axis=0)

        total = jnp.sum(lax.fori_loop(0, 16, part, total), axis=0, keepdims=True)
        for j in range(3):
            for h in range(2):
                val = jnp.where(yh == h, total[:, j * 128 : (j + 1) * 128], 0.0)
                sm[0, 2 + h : 3 + h, pl.ds(j * 256 + g * 128, 128)] = val

    def out_grads(g):
        res = dot_tn(xo[:, pl.ds(g * 512 + 384, 128)], cal[...]).astype(BF).reshape(2, 2, 2, 16, 1024)
        for h in range(2):
            for n in range(2):
                g_out[pl.ds(2 * g, 2), :, 2 * h + n] = res[:, :, h, :, n * 512 : (n + 1) * 512]

    def project(rows_of, src, w):
        def part(n):
            cs = at256(n)
            add_o = dot_nn(src[rows_of, pl.ds(384, 128)], wout[w, 0:128, cs]) + dot_nn(
                src[rows_of, pl.ds(896, 128)], wout[w, 128:256, cs]
            )
            outp[:, cs] += add_o
            add_g = dot_nt(src[rows_of, pl.ds(0, 384)], wqkv[w, 0, cs, :]) + dot_nt(
                src[rows_of, pl.ds(512, 384)], wqkv[w, 1, cs, :]
            )
            gnp[:, cs] += add_g

        loop(4, part)

    cot_s.wait_recv()
    nrm_s.wait_recv()
    ffn_tiles(0)
    ffn_grads(0)
    red0 = reduce_ffn(0)
    red0.step()
    ffn_tiles(1)
    ffn_grads(1)
    red1 = reduce_ffn(1)
    red1.step()
    red0.step()
    loop(4, ffn_out)
    qkv_block(own)
    qkv_block(sib)
    theirs = cal.at[at256(par), :]
    cot_p.wait_recv()
    cot_f = links.copy(theirs, theirs, sibling)
    cot_f.start()
    theirs = nal.at[at256(par), :]
    nrm_p.wait_recv()
    nrm_f = links.copy(theirs, theirs, sibling)
    nrm_f.start()
    qkv_block(par)
    cot_f.wait_recv()
    nrm_f.wait_recv()
    qkv_block(dia)
    for cp in (cot_s, nrm_s, cot_p, nrm_p, cot_f, nrm_f):
        cp.wait_send()

    attend(0, 3)
    red0.step()
    attend(0, 2)
    red1.step()
    attend(0, 1)
    attend(0, 0)
    send_back(0)
    qkv_grads(0)
    red2 = reduce_qkv(0)
    red2.step()
    red0.step()
    attend(1, 3)
    red0.step()
    red1.step()
    attend(1, 2)
    red2.step()
    attend(1, 1)
    red0.step()
    attend(1, 0)
    send_back(1)
    red1.step()
    qkv_grads(1)
    red3 = reduce_qkv(1)
    red3.step()
    for g in range(2):
        out_grads(g)
    red4 = reduce_out()
    red4.step()
    red2.step()
    project(here, xo, 0)
    red1.step()
    for g in range(2):
        bias_grads(g)
    red2.step()
    red3.step()
    red4.step()
    red1.step()

    for cp in back:
        cp.wait_recv()
    project(pl.ds(0, 512), xr, 1)
    stage = gh
    theirs_at, mine_at = (1 - c) * 256, c * 256
    rxs = R["rxs"]

    def stage_strip(u):
        r = pl.ds(pl.multiple_of(u * 64, 64), 64)
        rr = pl.ds(pl.multiple_of(theirs_at + u * 64, 64), 64)
        stage[r, :] = outp[rr, :].astype(BF)
        stage[pl.ds(pl.multiple_of(256 + u * 64, 64), 64), :] = gnp[rr, :].astype(BF)

    loop(4, stage_strip)
    swap = [links.copy(stage.at[pl.ds(w * 256, 256), :], rxs.at[w], sibling) for w in range(2)]
    for cp in swap:
        cp.start()
    red2.step()
    red3.step()
    red4.step()
    for cp in swap:
        cp.wait()

    def last_strip(u, carry):
        sg, sb = carry
        ru = pl.ds(pl.multiple_of(u * 32, 32), 32)
        r = pl.ds(pl.multiple_of(mine_at + u * 32, 32), 32)
        xin = tokens[ru, :].astype(F32)
        total = outp[r, :] + rxs[0, ru, :].astype(F32)
        o_out[ru, :] = (xin + total + vecs[2:3, :] + vecs[3:4, :]).astype(BF)
        gn = gnp[r, :] + rxs[1, ru, :].astype(F32)
        rs = mr[1, ru, 0:1]
        hat = (xin - mr[0, ru, 0:1]) * rs
        n = gn * gain
        grad = n - jnp.mean(n, axis=-1, keepdims=True) - hat * jnp.mean(n * hat, axis=-1, keepdims=True)
        o_tok[ru, :] = cot[ru, :].astype(F32) + grad * rs
        sg = sg + jnp.sum((gn * hat).reshape(4, 8, D), axis=0)
        sb = sb + jnp.sum(gn.reshape(4, 8, D), axis=0)
        return sg, sb

    zero = jnp.zeros((8, D), F32)
    sg, sb = lax.fori_loop(0, 8, last_strip, (zero, zero), unroll=2)
    sm[0, 5:6, :] = jnp.sum(sg, axis=0, keepdims=True)
    sm[0, 6:7, :] = jnp.sum(sb, axis=0, keepdims=True)

    def exchange(level, slot, devices):
        cps = [links.copy(sm.at[level], smr.at[slot + d], t) for d, t in enumerate(devices)]
        for cp in cps:
            cp.start()
        return cps

    def gather(level, slot, cps):
        for cp in cps:
            cp.wait()
        total = sm[level]
        for d in range(len(cps)):
            total = total + smr[slot + d]
        sm[level + 1] = total

    cps = exchange(0, 0, [at_z(d) for d in (1, 2, 3)])
    red3.step()
    red4.step()
    gather(0, 0, cps)
    cps = exchange(1, 3, [at_x(d) for d in (1, 2, 3)])
    red2.step()
    red3.step()
    red4.step()
    gather(1, 3, cps)
    cps = exchange(2, 6, [at_y(d) for d in (1, 2, 3)])
    red3.step()
    red4.step()
    gather(2, 6, cps)
    cps = exchange(3, 9, [sibling])
    for cp in cps:
        cp.wait()
    o_small[c] = sm[3]
    o_small[1 - c] = smr[9]
    for cp in back:
        cp.wait_send()
    for cp, sends, arrives in finals:
        if sends is None:
            cp.wait()
        else:
            pl.when(sends)(cp.wait_send)
            pl.when(arrives)(cp.wait_recv)
    for r in (red0, red1, red2, red3, red4):
        assert r.at == 6, r.at
    assert links.count <= NSEM, links.count


def hand_over(*refs):
    raw, small = refs[:6], refs[6]
    outs, vec, line = refs[7:13], refs[13:18], refs[18]
    for src, dst in zip(raw, outs):
        dst[...] = src[...]
    index = lax.axis_index("dp") * 4 + lax.axis_index("seq")
    for r, row in enumerate((5, 6, None, 4, None)):
        if row is not None:
            line[r : r + 1, 0:D] = small[0, row : row + 1, :] + small[1, row : row + 1, :]
    for t in range(4):
        line[4:5, t * 1024 : (t + 1) * 1024] = small[t % 2, t // 2 : t // 2 + 1, :]
        for j in range(3):
            line[2:3, pl.ds(j * 1024 + t * 256, 256)] = small[t % 2, 2 + t // 2 : 3 + t // 2, j * 256 : (j + 1) * 256]
    for r, out in enumerate(vec):
        n = out.shape[0]
        at = index * n
        part = line[r : r + 1, pl.ds(pl.multiple_of((at // 128) * 128, 128), 256)]
        part = pltpu.roll(jnp.broadcast_to(part, (8, 256)), (256 - at % 128) % 256, 1)
        out[...] = part[0, 0:n]


def on_device(tokens, lengths, ln_gain, ln_bias, w_qkv, b_qkv, w_out, b_out, w_in, b_in, w_down, b_down, cotangent):
    V = pl.BlockSpec(memory_space=pltpu.VMEM)
    H = pl.BlockSpec(memory_space=pl.ANY)
    S = pl.BlockSpec(memory_space=pltpu.SMEM)
    sds = jax.ShapeDtypeStruct
    outs = pl.pallas_call(
        kernel,
        out_shape=[
            sds((BLK, D), BF),
            sds((BLK, D), F32),
            sds((8, 3 * D), F32),
            sds((8, D), F32),
            sds((8, 4 * D), F32),
            sds((32, D), F32),
            sds((2, 8, 1024), F32),
        ],
        in_specs=[V] * 6 + [S, V, V, H, H, H, H],
        out_specs=[V] * 7,
        scratch_shapes=[pltpu.VMEM(shape, dt) for _, shape, dt in SCRATCH]
        + [pltpu.SemaphoreType.DMA((NSEM,)), pltpu.SemaphoreType.DMA((NSEM,)), pltpu.SemaphoreType.DMA((NLOC,))],
        compiler_params=pltpu.CompilerParams(collective_id=0, has_side_effects=True, vmem_limit_bytes=VMEM_LIMIT),
        name="layer",
    )(ln_gain, ln_bias, b_out, b_down, b_qkv, b_in, lengths, tokens[0], cotangent[0], w_qkv, w_out, w_in, w_down)
    vec = [sds((n // 128,), F32) for n in (D, D, 3 * D, D, 4 * D)]
    finals = pl.pallas_call(
        hand_over,
        out_shape=[sds(o.shape, o.dtype) for o in outs[:6]] + vec,
        in_specs=[V] * 7,
        out_specs=[V] * 11,
        scratch_shapes=[pltpu.VMEM((8, 4 * D + 128), F32)],
        name="shares",
    )(*outs)
    out, grad_tokens, g_wqkv, g_wout, g_win, g_wdn, g_gain, g_bias, g_bqkv, g_bout, g_bin = finals
    return (out[None], grad_tokens[None], g_gain, g_bias, g_wqkv, g_bqkv, g_wout, g_bout, g_win, g_bin, g_wdn, g_bout)


def solution(mesh):
    act, vec, mat = P("dp", "seq", None), P(("dp", "seq")), P(("dp", "seq"), None)
    return jax.shard_map(
        on_device,
        mesh=mesh,
        in_specs=(act, P("dp", None)) + (P(),) * 10 + (act,),
        out_specs=(act, act, vec, vec, mat, vec, mat, vec, mat, vec, mat, vec),
        check_vma=False,
    )
```

time: 219 us -> 121 us (0.55)
  Pallas kernels: 197 us -> 119 us
  local copies, waits for them, and re-layouts: 18.9 us -> 1.17 us
    pallas_call x1, Pallas kernels: 197 us -> 116 us  [on_device(): pl.pallas_call(kernel, out_shape=[sds((BLK, D), BF), sds((BLK, D), F32),...]
    unnamed x16 -> x1, local copies, waits for them, and re-layouts: 14.9 us -> 1.17 us
    pallas_call x0 -> x1, Pallas kernels: none -> 2.9 us  [on_device(): pl.pallas_call(hand_over, out_shape=[sds(o.shape, o.dtype) for o in outs[...]
    dynamic_slice x5 -> x0, local copies, waits for them, and re-layouts: 2.42 us -> none  [share(): return lax.dynamic_slice_in_dim(vec, index * n, n)]
where the time goes in v2:
time: 121 us; the launch traced here: 120 us
  Pallas kernels  119 us (98%)
    pallas_call x1, Pallas kernels, on_device(): pl.pallas_call(kernel, out_shape=[sds((BLK, D), BF), sds((BLK, D), F32),...  116 us
    pallas_call x1, Pallas kernels, on_device(): pl.pallas_call(hand_over, out_shape=[sds(o.shape, o.dtype) for o in outs[...  2.9 us

profile of v2, /device:TPU:1, one launch (start us, length us, event | category | flops | bytes accessed | tf_op | source)
XLA Modules:
  0.0 120.4 jit_solution(2594038272424110756)
XLA Ops:
  0.6 115.7 %layer.1 = (bf16[256,1024]{1,0:T(8,128)(2,1)}, f32[256,1024]{1,0:T(8,128)}, f32[8,3072]{1,0:T(8,128)}, f32[8,1024]{1,0:T(8,128)}, f32[8,4096]{1,0:T(8,128)}, /*index=5*/f32[32,1024]{1,0:T(8,128)}, f32[2,8,1024]{2,1,0:T(8,128)}) custom-call(bf16[1024]{0:T(1024)(128)(2,1)} %refs_0_.1, bf16[1024]{0:T(1024)(128)(2,1)} %refs_1_.1, bf16[1024]{0:T(1024)(128)(2,1)} %refs_2_.1, ...), custom_call_target="tpu_custom_call" | custom-call | tf_op jit(solution)/shard_map/layer/pallas_call | solution.py:816
  116.4 2.9 %shares.1 = (bf16[256,1024]{1,0:T(8,128)(2,1)}, f32[256,1024]{1,0:T(8,128)}, f32[8,3072]{1,0:T(8,128)}, f32[8,1024]{1,0:T(8,128)}, f32[8,4096]{1,0:T(8,128)}, /*...) custom-call(bf16[256,1024]{1,0:T(8,128)(2,1)} %get-tuple-element.30.refs_0_,, ...), custom_call_target="tpu_custom_call" | custom-call | tf_op jit(solution)/shard_map/shares/pallas_call | solution.py:835
  119.3 1.2 copy.26

commit v3 on v2

v3 whole, which is shorter than its diff:
```python
import math

import jax
import jax.numpy as jnp
from jax import lax
from jax.experimental import pallas as pl
from jax.experimental.pallas import tpu as pltpu
from jax.sharding import PartitionSpec as P

HEAD = 64
ROT = 16
ROW = 1024
D = 1024
BLK = 256
BF = jnp.bfloat16
F32 = jnp.float32
MESH = pl.DeviceIdType.MESH
VMEM_LIMIT = 63 * 2**20


def dot_nn(a, b):
    return lax.dot_general(a, b, (((1,), (0,)), ((), ())), preferred_element_type=F32)


def dot_nt(a, b):
    return lax.dot_general(a, b, (((1,), (1,)), ((), ())), preferred_element_type=F32)


def dot_tn(a, b):
    return lax.dot_general(a, b, (((0,), (0,)), ((), ())), preferred_element_type=F32)


def loop(count, step):
    def run(i, carry):
        step(i)
        return carry

    lax.fori_loop(0, count, run, 0)


def at256(i):
    return pl.ds(pl.multiple_of(i * 256, 256), 256)


SCRATCH = [
    ("vecs", (16, D), F32),
    ("win", (2, D, 1024), BF),
    ("wdn", (2, 1024, D), BF),
    ("wqkv", (2, 2, D, 384), BF),
    ("wout", (2, BLK, D), BF),
    ("nall", (ROW, D), BF),
    ("call", (ROW, D), BF),
    ("kt", (2, 128, ROW), BF),
    ("vt", (2, 128, ROW), BF),
    ("qh", (2, BLK, 128), BF),
    ("doh", (2, BLK, 128), BF),
    ("act", (ROW, 1024), BF),
    ("gh", (ROW, 1024), BF),
    ("g_ffn", (2, 2, 4, 4, 4, 16, 1024), BF),
    ("g_qkv", (2, 4, 2, 4, 32, 384), BF),
    ("g_out", (4, 2, 4, 16, 512), BF),
    ("outp", (512, D), F32),
    ("gnp", (512, D), F32),
    ("xo", (ROW, 1024), BF),
    ("pb", (2, ROW, BLK), BF),
    ("ds", (2, ROW, BLK), BF),
    ("dk", (ROW, 128), F32),
    ("dv", (ROW, 128), F32),
    ("dq", (128, BLK), F32),
    ("mx", (128, BLK), F32),
    ("xr", (512, 1024), BF),
    ("tab", (2, ROW, 128), F32),
    ("mr", (2, BLK, 128), F32),
    ("sm", (2, 8, 1024), F32),
    ("smr", (22, 8, 1024), F32),
    ("ln", (2, 8, 256), F32),
    ("lnr", (22, 8, 256), F32),
    ("rxs", (2, BLK, D), BF),
    ("r1z_ffn", (2, 6, 2, 4, 2, 16, 512), BF),
    ("r1x_ffn", (2, 6, 2, 2, 4, 16, 512), BF),
    ("r2_ffn", (2, 2, 6, 2, 2, 16, 512), BF),
    ("r3_ffn", (2, 3, 2, 16, 1024), BF),
    ("r1z_qkv", (2, 6, 4, 32, 256), BF),
    ("r1x_qkv", (2, 6, 4, 32, 256), BF),
    ("r2_qkv", (2, 2, 7, 32, 256), BF),
    ("r1z_out", (6, 4, 16, 256), BF),
    ("r1x_out", (6, 4, 16, 256), BF),
    ("r2_out", (2, 7, 16, 256), BF),
    ("fin_ffn", (2, 2, 16, 1024), F32),
    ("fin_qkv", (2, 32, 384), F32),
    ("fin_out", (16, 512), F32),
]
PIECE = 32
NSEM = 384
NLOC = 24


class Links:
    def __init__(self, send, recv):
        self.send, self.recv, self.count = send, recv, 0

    def copy(self, src, dst, device):
        k = self.count
        self.count += 1
        return pltpu.make_async_remote_copy(
            src_ref=src,
            dst_ref=dst,
            send_sem=self.send.at[k],
            recv_sem=self.recv.at[k],
            device_id=device,
            device_id_type=MESH,
        )


class Pieces:
    def __init__(self, links, src, dst, device, rows):
        self.whole = links.copy(src, dst, device)
        k = links.count - 1
        self.parts = []
        for at in range(0, src.shape[0], rows):
            part = pl.ds(at, rows)
            links.count = k
            self.parts.append(links.copy(src.at[part], dst.at[part], device))
        self.wait, self.wait_send, self.wait_recv = self.whole.wait, self.whole.wait_send, self.whole.wait_recv

    def start(self):
        for cp in self.parts:
            cp.start()


def add_into(dst, sources):
    if len(dst.shape) > 2:
        for i in range(dst.shape[0]):
            add_into(dst.at[i], [s.at[i] for s in sources])
        return
    total = dst[...].astype(F32)
    for s in sources:
        total = total + s[...].astype(F32)
    dst[...] = total.astype(dst.dtype)


class Ring:
    def __init__(self, links, block, pos, right, left, land):
        self.block, self.land = block, land
        self.pos = pos
        self.rt, self.lf, self.opp = (pos + 1) % 4, (pos + 3) % 4, (pos + 2) % 4
        c = links.copy
        self.early = [
            c(block(self.opp, 0), land.at[0], right),
            c(block(self.opp, 1), land.at[1], left),
            c(block(self.rt, 1), land.at[2], right),
            c(block(self.lf, 0), land.at[3], left),
        ]
        self.late = [
            c(block(self.rt, 0), land.at[4], right),
            c(block(self.lf, 1), land.at[5], left),
        ]

    def start(self):
        for c in self.early:
            c.start()

    def middle(self):
        self.early[0].wait_recv()
        add_into(self.block(self.rt, 0), [self.land.at[0]])
        self.late[0].start()
        self.early[1].wait_recv()
        add_into(self.block(self.lf, 1), [self.land.at[1]])
        self.late[1].start()

    def finish(self):
        for c in self.early[2:] + self.late:
            c.wait_recv()
        add_into(self.block(self.pos, 0), [self.land.at[4], self.land.at[3]])
        add_into(self.block(self.pos, 1), [self.land.at[2], self.land.at[5]])
        for c in self.early + self.late:
            c.wait_send()


class Reduce:
    def __init__(self, links, ref, lands, pos, at_z, at_x, last, after, col, width):
        z, x, y = pos
        every = slice(None)
        first, second = pl.ds(col, width // 2), pl.ds(col + width // 2, width // 2)
        land1z, land1x, land2z, land2x, self.land_y = lands

        def view(a, h, b, cols):
            return ref.at[a, pl.ds(h * 2, 2), b, every, cols]

        zr, zl, xr, xl = at_z(1), at_z(3), at_x(1), at_x(3)
        self.one = [
            Ring(links, lambda t, h: view(every, h, t, first), z, zr, zl, land1z),
            Ring(links, lambda t, h: view(t, h, every, second), x, xr, xl, land1x),
        ]
        self.two = [
            Ring(links, lambda t, h: view(t, h, z, first), x, xr, xl, land2z),
            Ring(links, lambda t, h: view(x, h, t, second), z, zr, zl, land2x),
        ]
        both = pl.ds(col, width)
        self.own = ref.at[x, y, z, every, both]
        self.last = [links.copy(ref.at[x, ty, z, every, both], self.land_y.at[n], d) for n, (ty, d) in enumerate(last)]
        self.after = after
        self.at = 0

    def result_into(self, dst):
        total = self.own[...].astype(F32)
        for n in range(3):
            total = total + self.land_y[n].astype(F32)
        dst[...] = total

    def step(self):
        one, two = self.one, self.two
        if self.at == 0:
            for r in one:
                r.start()
        elif self.at == 1:
            for r in one:
                r.middle()
        elif self.at == 2:
            for r, n in zip(one, two):
                r.finish()
            for n in two:
                n.start()
        elif self.at == 3:
            for r in two:
                r.middle()
        elif self.at == 4:
            for r in two:
                r.finish()
            for cp in self.last:
                cp.start()
        elif self.at == 5:
            for cp in self.last:
                cp.wait()
            self.after(self)
        self.at += 1


class ReduceShort:
    def __init__(self, links, ref, lands, pos, at_z, at_x, far, after, half):
        z, x, yl = pos
        every = slice(None)
        cols = (pl.ds(0, half), pl.ds(half, ref.shape[-1] - half))
        land1z, land1x, land2z, land2x = lands
        self.one = [
            Ring(links, lambda t, h: ref.at[every, h, t, every, cols[0]], z, at_z(1), at_z(3), land1z),
            Ring(links, lambda t, h: ref.at[t, h, every, every, cols[1]], x, at_x(1), at_x(3), land1x),
        ]
        self.own = [ref.at[x, yl, z, :, c] for c in cols]
        self.lands = (land2z, land2x)
        self.two = [
            [links.copy(ref.at[tx, ty, z, :, cols[0]], land2z.at[n], d) for n, (tx, ty, d) in enumerate(far[0])],
            [links.copy(ref.at[x, ty, tz, :, cols[1]], land2x.at[n], d) for n, (tz, ty, d) in enumerate(far[1])],
        ]
        self.cols, self.after, self.at = cols, after, 0

    def step(self):
        if self.at == 0:
            for r in self.one:
                r.start()
        elif self.at == 1:
            for r in self.one:
                r.middle()
        elif self.at == 2:
            for r, cps in zip(self.one, self.two):
                r.finish()
                for cp in cps:
                    cp.start()
        elif self.at == 3:
            for cps in self.two:
                for cp in cps:
                    cp.wait()
            self.after(self)
        self.at += 1

    def result_into(self, dst):
        for own, land, cols in zip(self.own, self.lands, self.cols):
            total = own[...].astype(F32)
            for n in range(7):
                total = total + land[n].astype(F32)
            dst[:, cols] = total


def kernel(*refs):
    small, (lens, tokens, cot, w_qkv, w_out, w_in, w_down) = refs[:6], refs[6:13]
    (o_out, o_tok, o_wqkv, o_wout, o_win, o_wdn, o_small, o_ln) = refs[13:21]
    rest = refs[21:]
    R = {name: r for (name, _, _), r in zip(SCRATCH, rest)}
    send, recv, loc = rest[len(SCRATCH) :]
    links = Links(send, recv)

    dpi, s = lax.axis_index("dp"), lax.axis_index("seq")
    z, x, yl = dpi // 8, (dpi // 2) % 4, dpi % 2
    yh, c = s // 2, s % 2
    y, y_other = yh * 2 + yl, yh * 2 + 1 - yl

    def dev(zz, xx, yy, cc):
        return ((zz % 4) * 8 + (xx % 4) * 2 + (yy % 4) % 2, ((yy % 4) // 2) * 2 + cc)

    def at_z(d):
        return dev(z + d, x, y, c)

    def at_x(d):
        return dev(z, x + d, y, c)

    def at_y(d):
        return dev(z, x, y + d, c)

    sibling = dev(z, x, y, 1 - c)
    partner = dev(z, x, y + 2, c)
    diagonal = dev(z, x, y + 2, 1 - c)

    meet = [at_x(d) for d in (1, 2, 3)] + [at_y(d) for d in (1, 2, 3)] + [sibling, diagonal]
    for d in (1, 2, 3):
        for cc in (c, 1 - c):
            meet += [dev(z + d, x, y, cc), dev(z + d, x, y + 2, cc)]
    plane = [(dz, dx) for dz in range(4) for dx in range(4) if dz or dx]
    meet += [dev(z + dz, x + dx, y, c) for dz, dx in plane if dz and dx]
    for d in (1, 2, 3):
        meet += [dev(z + d, x, y_other, c), dev(z, x + d, y_other, c)]
    meet += [dev(z, x, y + 1, 1 - c), dev(z, x, y + 3, 1 - c)]
    barrier = pltpu.get_barrier_semaphore()
    for d in meet:
        pl.semaphore_signal(barrier, inc=1, device_id=d, device_id_type=MESH)

    loads = []

    def load(src, dst):
        cp = pltpu.make_async_copy(src, dst, loc.at[len(loads)])
        cp.start()
        loads.append(cp)

    for w, sw in enumerate((s, (1 - yh) * 2 + c)):
        load(w_out.at[at256(sw), :], R["wout"].at[w])
    for a in range(2):
        for h in range(2):
            wide = pl.ds(pl.multiple_of((2 * a + c) * 1024 + h * 512, 512), 512)
            load(w_in.at[:, wide], R["win"].at[a, :, pl.ds(h * 512, 512)])
            load(w_down.at[wide, :], R["wdn"].at[a, pl.ds(h * 512, 512), :])
    for w, sw in enumerate((s, (1 - yh) * 2 + c)):
        for g in range(2):
            for j in range(3):
                cols = pl.ds(pl.multiple_of(j * 1024 + sw * 256 + g * 128, 128), 128)
                load(w_qkv.at[:, cols], R["wqkv"].at[w, g, :, pl.ds(j * 128, 128)])

    def loaded(first, count):
        for cp in loads[first : first + count]:
            cp.wait()

    own, sib = s, yh * 2 + 1 - c
    par, dia = (1 - yh) * 2 + c, (1 - yh) * 2 + 1 - c
    cal, nal = R["call"], R["nall"]
    cot_s = Pieces(links, cot, cal.at[at256(own), :], sibling, PIECE)
    cot_p = links.copy(cot, cal.at[at256(own), :], partner)
    cal[at256(own), :] = cot[...]

    vecs, row = R["vecs"], 0
    for ref in small:
        for i in range(ref.shape[0] // D):
            vecs[row : row + 1, :] = ref[pl.ds(i * D, D)].astype(F32).reshape(1, D)
            row += 1
    gain, shift = vecs[0:1, :], vecs[1:2, :]
    mr = R["mr"]

    def norm_strip(u, carry):
        rows = pl.ds(pl.multiple_of(u * 32, 32), 32)
        xin = tokens[rows, :].astype(F32)
        mean = jnp.mean(xin, axis=-1, keepdims=True)
        cen = xin - mean
        r = lax.rsqrt(jnp.mean(cen * cen, axis=-1, keepdims=True) + 1e-05)
        mr[0, rows, :] = jnp.broadcast_to(mean, (32, 128))
        mr[1, rows, :] = jnp.broadcast_to(r, (32, 128))
        nal[pl.ds(pl.multiple_of(own * 256 + u * 32, 32), 32), :] = (cen * r * gain + shift).astype(BF)
        return carry

    lax.fori_loop(0, 8, norm_strip, 0, unroll=2)
    mine = nal.at[at256(own), :]
    nrm_s = Pieces(links, mine, mine, sibling, PIECE)
    nrm_p = links.copy(mine, mine, partner)
    pl.semaphore_wait(barrier, len(meet))
    for cp in (cot_s, nrm_s, nrm_p):
        cp.start()

    sm, smr = R["sm"], R["smr"]
    sm[0] = jnp.zeros((8, 1024), F32)
    sm[0, 4:5, :] = jnp.sum(cot[...].astype(F32), axis=0, keepdims=True)

    start1 = lens[0, 0]
    start2 = start1 + lens[0, 1]
    start3 = start2 + lens[0, 2]

    def first_of(t):
        return jnp.where(t >= start3, start3, jnp.where(t >= start2, start2, jnp.where(t >= start1, start1, 0)))

    tab = R["tab"]

    def tables(u):
        rows = pl.ds(pl.multiple_of(u * 64, 64), 64)
        t = lax.broadcasted_iota(jnp.int32, (64, 128), 0) + u * 64
        lane = lax.broadcasted_iota(jnp.int32, (64, 128), 1) % HEAD
        offset = (t - first_of(t)).astype(F32)
        freq = jnp.zeros((64, 128), F32)
        for i in range(ROT // 2):
            freq = jnp.where(lane % (ROT // 2) == i, math.exp(-2.0 * i * math.log(10000.0) / ROT), freq)
        angle = offset * freq
        cosine, sine = jnp.cos(angle), jnp.sin(angle)
        tab[0, rows, :] = jnp.where(lane < ROT, cosine, 1.0)
        tab[1, rows, :] = jnp.where(lane < ROT // 2, -sine, jnp.where(lane < ROT, sine, 0.0))

    def tables_():
        loop(16, tables)

    low_lane = lax.broadcasted_iota(jnp.int32, (BLK, 128), 1) % HEAD < ROT // 2

    def rotate(val, rows, sign):
        other = jnp.where(low_lane, pltpu.roll(val, 128 - ROT // 2, 1), pltpu.roll(val, ROT // 2, 1))
        return val * tab[0, rows, :] + sign * other * tab[1, rows, :]

    win, wdn, wqkv, wout = R["win"], R["wdn"], R["wqkv"], R["wout"]
    act, gh, outp, gnp = (R[n] for n in ("act", "gh", "outp", "gnp"))
    hid, ga = outp.at[:, pl.ds(0, 256)], gnp.at[:, pl.ds(0, 256)]
    kt, vt, qh, doh = (R[n] for n in ("kt", "vt", "qh", "doh"))
    xo, xr = R["xo"], R["xr"]
    q, k, v, do = ([xo.at[:, pl.ds(g * 512 + j * 128, 128)] for g in range(2)] for j in range(4))

    def qkv_block(blk):
        rows = at256(blk)
        for g in range(2):
            yv = dot_nn(nal[rows, :], wqkv[0, g])
            for j, dst in enumerate((q, k, v)):
                b = vecs[4 + j : 5 + j, pl.ds(pl.multiple_of(s * 256 + g * 128, 128), 128)]
                part = yv[:, j * 128 : (j + 1) * 128] + b
                if j < 2:
                    part = rotate(part, rows, 1.0)
                part = part.astype(BF)
                dst[g][rows, :] = part * jnp.asarray(0.125, BF) if j == 0 else part
                if j > 0:
                    (kt, vt)[j - 1][g, :, rows] = jnp.transpose(part)

    here = pl.ds(pl.multiple_of(yh * 512, 512), 512)
    there = pl.ds(pl.multiple_of((1 - yh) * 512, 512), 512)

    def grad_mixed(rows):
        for w, (dst, at) in enumerate(((do, rows), (q, pl.ds(pl.multiple_of(rows.start + (1 - 2 * yh) * 512, 256), 256)))):
            d = dot_nt(cal[rows, :], wout[w]).astype(BF)
            for g in range(2):
                dst[g][at, :] = d[:, g * 128 : (g + 1) * 128]

    def tile(a, t, at, count):
        cs = at256(t)
        near = pl.ds(pl.multiple_of(at, 256), count)
        rows = pl.ds(pl.multiple_of(yh * 512 + at, 256), count)
        hid[near, :] = dot_nn(nal[rows, :], win[a, :, cs]) + vecs[pl.ds(7 + 2 * a + c, 1), cs]
        ga[near, :] = dot_nt(cal[rows, :], wdn[a, cs, :])

        def strip(u, total):
            r = pl.ds(pl.multiple_of(at + u * 32, 32), 32)
            h = hid[r, :]
            cdf = 0.5 + 0.5 * lax.erf(h * (1.0 / math.sqrt(2.0)))
            dens = jnp.exp(-0.5 * h * h) * (1.0 / math.sqrt(2.0 * math.pi))
            to = pl.ds(pl.multiple_of(a * 512 + at + u * 32, 32), 32)
            act[to, cs] = (h * cdf).astype(BF)
            grad = (ga[r, :] * (cdf + h * dens)).astype(BF)
            gh[to, cs] = grad
            return total + jnp.sum(grad.astype(F32).reshape(4, 8, 256), axis=0)

        total = lax.fori_loop(0, count // 32, strip, jnp.zeros((8, 256), F32), unroll=2)
        sm[0, a : a + 1, cs] += jnp.sum(total, axis=0, keepdims=True)

    def tiles(a, h):
        loaded(2 + 4 * a + 2 * h, 2)
        loop(2, lambda i: tile(a, 2 * h + i, 0, 512))

    g_ffn = R["g_ffn"]

    def grads_in(a, h):
        half = pl.ds(a * 512, 512)

        def part(m):
            res = dot_tn(nal[here, at256(m)], gh[half, pl.ds(h * 512, 512)]).astype(BF)
            g_ffn[a, 0, :, :, m, :, pl.ds(h * 512, 512)] = res.reshape(4, 4, 16, 512)

        loop(4, part)

    def grads_down(a):
        half = pl.ds(a * 512, 512)

        def part(m):
            res = dot_tn(act[half, at256(m)], cal[here, :]).astype(BF)
            g_ffn[a, 1, m] = res.reshape(4, 4, 16, 1024)

        loop(4, part)

    def ffn_out(n):
        cs = at256(n)
        top, low = pl.ds(0, 512), pl.ds(512, 512)
        outp[:, cs] = dot_nn(act[top, :], wdn[0, :, cs]) + dot_nn(act[low, :], wdn[1, :, cs])
        gnp[:, cs] = dot_nt(gh[top, :], win[0, cs, :]) + dot_nt(gh[low, :], win[1, cs, :])

    finals = []

    def put(src, dst, device, sends=None, arrives=None):
        cp = links.copy(src, dst, device)
        finals.append((cp, sends, arrives))
        if sends is None:
            cp.start()
        else:
            pl.when(sends)(cp.start)

    def keep(src, dst, here_too):
        @pl.when(here_too)
        def _():
            dst[...] = src[...]

    fin_ffn, fin_qkv, fin_out = R["fin_ffn"], R["fin_qkv"], R["fin_out"]

    def in_done(a, col, width):
        def done(red):
            cols = pl.ds(pl.multiple_of((2 * a + c) * 1024 + col, 512), width)
            fin = fin_ffn.at[a, 0, :, pl.ds(col, width)]
            red.result_into(fin)
            put(fin.at[pl.ds(pl.multiple_of((1 - c) * 8, 8), 8), :], o_win.at[:, cols], sibling)
            o_win[:, cols] = fin[pl.ds(pl.multiple_of(c * 8, 8), 8), :]

        return done

    def down_done(a):
        def done(red):
            red.result_into(fin_ffn.at[a, 1])
            to = dev(2 * a + c, x, y, z // 2)
            for h in range(2):
                rows, right = pl.ds(h * 16, 16), z % 2 == h
                here_too = (z == 2 * a + c) & (z // 2 == c)
                from_here = (z == 2 * c + h) & (z % 2 == c)
                sends = right & jnp.logical_not(here_too)
                arrives = (z // 2 == a) & jnp.logical_not(from_here)
                put(fin_ffn.at[a, 1], o_wdn.at[rows, :], to, sends, arrives)
                keep(fin_ffn.at[a, 1], o_wdn.at[rows, :], right & here_too)

        return done

    def qkv_done(g):
        def done(red):
            red.result_into(fin_qkv.at[g])
            for j in range(3):
                src_l = pl.ds(j * 128, 128)
                dst_l = pl.ds(pl.multiple_of(j * 1024 + s * 256 + g * 128, 128), 128)
                for d in (1, 2, 3):
                    t = (s + d) % 4
                    put(fin_qkv.at[g, pl.ds(pl.multiple_of(t * 8, 8), 8), src_l], o_wqkv.at[:, dst_l], (dpi, t))
                o_wqkv[:, dst_l] = fin_qkv[g, pl.ds(pl.multiple_of(s * 8, 8), 8), src_l]

        return done

    def out_done(red):
        red.result_into(fin_out)
        for cc in range(2):
            to = dev(s, x, (z // 2) * 2 + yl, cc)
            src = fin_out.at[pl.ds(cc * 8, 8), :]
            for h in range(2):
                dst, right = o_wout.at[:, pl.ds(h * 512, 512)], z % 2 == h
                here_too = (z == s) & (z // 2 == yh) & (c == cc)
                from_here = (z == 2 * yh + h) & (s == z)
                sends = right & jnp.logical_not(here_too)
                arrives = (c == cc) & jnp.logical_not(from_here)
                put(src, dst, to, sends, arrives)
                keep(src, dst, right & here_too)

    def place(yy):
        return (yy % 2) * 2 + (yy % 4) // 2

    def reduce_ffn(a, w, col, width, done):
        last = [(place(y + d), at_y(d)) for d in (1, 2, 3)]
        half = pl.ds(col // 2, width // 2)
        lands = (R["r1z_ffn"].at[a, :, w, :, :, :, half], R["r1x_ffn"].at[a, :, w, :, :, :, half])
        lands += (R["r2_ffn"].at[a, 0, :, w, :, :, half], R["r2_ffn"].at[a, 1, :, w, :, :, half])
        lands += (R["r3_ffn"].at[a, :, w, :, pl.ds(col, width)],)
        return Reduce(links, g_ffn.at[a, w], lands, (z, x, place(y)), at_z, at_x, last, done, col, width)

    def reduce_in(a, col, width):
        return reduce_ffn(a, 0, col, width, in_done(a, col, width))

    def reduce_down(a):
        return reduce_ffn(a, 1, 0, 1024, down_done(a))

    def reduce_qkv(g):
        half = 256 if g == 0 else 128
        one, two = pl.ds(0, half), pl.ds(0, 384 - half)
        lands = (R["r1z_qkv"].at[g, :, :, :, one], R["r1x_qkv"].at[g, :, :, :, two])
        lands += (R["r2_qkv"].at[g, 0, :, :, one], R["r2_qkv"].at[g, 1, :, :, two])
        return ReduceShort(links, R["g_qkv"].at[g], lands, (z, x, yl), at_z, at_x, far, qkv_done(g), half)

    def reduce_out():
        lands = (R["r1z_out"], R["r1x_out"], R["r2_out"].at[0], R["r2_out"].at[1])
        return ReduceShort(links, R["g_out"], lands, (z, x, yl), at_z, at_x, far, out_done, 256)

    far = [
        [((x + d) % 4, ty, dev(z, x + d, ry, c)) for d in range(4) for ty, ry in ((yl, y), (1 - yl, y_other)) if d or ty is not yl],
        [((z + d) % 4, ty, dev(z + d, x, ry, c)) for d in range(4) for ty, ry in ((yl, y), (1 - yl, y_other)) if d or ty is not yl],
    ]

    pb, ds = R["pb"], R["ds"]
    dk, dv, dq, mx = (R[n] for n in ("dk", "dv", "dq", "mx"))
    g_qkv, g_out = R["g_qkv"], R["g_out"]

    def attend(g, i):
        n = 256 * (i + 1)
        rows = pl.ds(256 * i, 256)
        keys = pl.ds(0, n)
        chunks = [pl.ds(j * 256, 256) for j in range(n // 256)]

        def sc(u, ch):
            return outp.at[pl.ds(u * 256, 256), ch]

        def dp(u, ch):
            return gnp.at[pl.ds(u * 256, 256), ch]

        def fold(a, op):
            return op(a.reshape(32, 8, BLK), axis=0)

        tq = lax.broadcasted_iota(jnp.int32, (1, BLK), 1) + 256 * i
        first_key = first_of(tq)

        def allowed(j):
            tk = lax.broadcasted_iota(jnp.int32, (BLK, BLK), 0) + 256 * j
            return (tk >= first_key) & (tk <= tq) if j == i else tk >= first_key

        heads = range(2)
        tops, stats = [], []
        for u in heads:
            lanes = lax.broadcasted_iota(jnp.int32, (BLK, 128), 1) // HEAD == u
            qh[u] = jnp.where(lanes, q[g][rows, :], jnp.zeros((), BF))
            doh[u] = jnp.where(lanes, do[g][rows, :], jnp.zeros((), BF))
        for u in heads:
            top = jnp.full((8, BLK), -1e30, F32)
            for j, ch in enumerate(chunks):
                a = jnp.where(allowed(j), dot_nt(k[g][ch, :], qh[u]), -1e30)
                sc(u, ch)[...] = a
                top = jnp.maximum(top, fold(a, jnp.max))
            tops.append(jnp.max(top, axis=0, keepdims=True))
        for u in heads:
            total, inner = jnp.zeros((8, BLK), F32), jnp.zeros((8, BLK), F32)
            for ch in chunks:
                gr = dot_nt(v[g][ch, :], doh[u])
                dp(u, ch)[...] = gr
                e = jnp.exp(sc(u, ch)[...] - tops[u])
                sc(u, ch)[...] = e
                total, inner = total + fold(e, jnp.sum), inner + fold(e * gr, jnp.sum)
            inv = 1.0 / jnp.sum(total, axis=0, keepdims=True)
            stats.append((inv, jnp.sum(inner, axis=0, keepdims=True) * inv))
        for u in heads:
            inv, inner = stats[u]
            for j, ch in enumerate(chunks):
                p = sc(u, ch)[...] * inv
                p_low = p.astype(BF)
                d_low = (p * (dp(u, ch)[...] - inner)).astype(BF)
                pb[u, ch, :] = p_low
                ds[u, ch, :] = d_low
                if i == 3 and u == 0:
                    dk[ch, :] = dot_nn(d_low, qh[u])
                    dv[ch, :] = dot_nn(p_low, doh[u])
                else:
                    dk[ch, :] += dot_nn(d_low, qh[u])
                    dv[ch, :] += dot_nn(p_low, doh[u])
        for u in heads:
            hr = pl.ds(u * HEAD, HEAD)
            mx[hr, :] = dot_nn(vt[g, hr, keys], pb[u, keys, :])
            dq[hr, :] = dot_nn(kt[g, hr, keys], ds[u, keys, :])

        def place_in(j, val):
            xo[rows, pl.ds(g * 512 + j * 128, 128)] = val

        place_in(3, jnp.transpose(mx[...]).astype(BF))
        grad_q = jnp.transpose(dq[...] * 0.125).astype(BF).astype(F32)
        place_in(0, rotate(grad_q, rows, -1.0).astype(BF))
        grad_k = dk[rows, :].astype(BF).astype(F32)
        place_in(1, rotate(grad_k, rows, -1.0).astype(BF))
        place_in(2, dv[rows, :].astype(BF))

    back = []

    def send_back(g):
        cols = pl.ds(g * 512, 512)
        cp = links.copy(xo.at[there, cols], xr.at[:, cols], partner)
        cp.start()
        back.append(cp)

    def qkv_grads(g):
        def part(m):
            res = dot_tn(nal[:, at256(m)], xo[:, pl.ds(g * 512, 384)]).astype(BF)
            g_qkv[g, :, :, m] = res.reshape(4, 2, 32, 384)

        loop(4, part)

    def bias_grads(g):
        total = jnp.zeros((8, 384), F32)

        def part(u, total):
            r = pl.ds(pl.multiple_of(u * 64, 64), 64)
            return total + jnp.sum(xo[r, pl.ds(g * 512, 384)].astype(F32).reshape(8, 8, 384), axis=0)

        total = jnp.sum(lax.fori_loop(0, 16, part, total), axis=0, keepdims=True)
        for j in range(3):
            for h in range(2):
                val = jnp.where(yh == h, total[:, j * 128 : (j + 1) * 128], 0.0)
                sm[0, 2 + h : 3 + h, pl.ds(j * 256 + g * 128, 128)] = val

    def out_grads(g):
        res = dot_tn(xo[:, pl.ds(g * 512 + 384, 128)], cal[...]).astype(BF).reshape(2, 2, 2, 16, 1024)
        for h in range(2):
            for n in range(2):
                g_out[pl.ds(2 * g, 2), :, 2 * h + n] = res[:, :, h, :, n * 512 : (n + 1) * 512]

    mine_at, theirs_at = c * 256, (1 - c) * 256

    def project(src, base, w, pairs, at):
        dst = pl.ds(pl.multiple_of(at, 256), 256)
        rows = pl.ds(pl.multiple_of(base + at, 256), 256)

        def part(n):
            cs = at256(n)
            add_o, add_g = outp[dst, cs], gnp[dst, cs]
            for g in pairs:
                add_o += dot_nn(src[rows, pl.ds(g * 512 + 384, 128)], wout[w, pl.ds(g * 128, 128), cs])
                add_g += dot_nt(src[rows, pl.ds(g * 512, 384)], wqkv[w, g, cs, :])
            outp[dst, cs], gnp[dst, cs] = add_o, add_g

        loop(4, part)

    stage, rxs = gh, R["rxs"]

    def stage_strip(u):
        r = pl.ds(pl.multiple_of(u * 64, 64), 64)
        rr = pl.ds(pl.multiple_of(theirs_at + u * 64, 64), 64)
        stage[r, :] = outp[rr, :].astype(BF)
        stage[pl.ds(pl.multiple_of(256 + u * 64, 64), 64), :] = gnp[rr, :].astype(BF)

    pairs_y = [at_y(d) for d in (1, 2, 3)] + [dev(z, x, y + d, 1 - c) for d in range(4)]
    plane_devices = [dev(z + dz, x + dx, y, c) for dz, dx in plane]
    early, late = (sm, smr), (R["ln"], R["lnr"])

    def exchange(level, slot, bufs, devices):
        cps = [links.copy(bufs[0].at[level], bufs[1].at[slot + d], t) for d, t in enumerate(devices)]
        for cp in cps:
            cp.start()
        return cps

    def plane_sum(bufs, cps):
        for cp in cps:
            cp.wait()
        total = bufs[0][0]
        for d in range(len(cps)):
            total = total + bufs[1][d]
        bufs[0][1] = total

    def finish_sums(bufs, cps, out):
        for cp in cps:
            cp.wait()
        same, other = bufs[0][1], bufs[1][18]
        for d in range(3):
            same = same + bufs[1][15 + d]
            other = other + bufs[1][19 + d]
        out[c], out[1 - c] = same, other

    def send_grad_mixed():
        for g in range(2):
            cp = links.copy(q[g].at[there, :], do[g].at[here, :], partner)
            cp.start()
            back_do.append(cp)

    back_do = []

    def forward(buf):
        rows = buf.at[at256(par), :]
        cp = Pieces(links, rows, rows, sibling, PIECE)
        cp.start()
        return cp

    def sum_strip(u, carry):
        sg, sb = carry
        ru = pl.ds(pl.multiple_of(u * 32, 32), 32)
        r = pl.ds(pl.multiple_of(mine_at + u * 32, 32), 32)
        gn = gnp[r, :] + rxs[1, ru, :].astype(F32)
        gnp[r, :] = gn
        hat = (tokens[ru, :].astype(F32) - mr[0, ru, 0:1]) * mr[1, ru, 0:1]
        return sg + jnp.sum((gn * hat).reshape(4, 8, D), axis=0), sb + jnp.sum(gn.reshape(4, 8, D), axis=0)

    def norm_sums():
        zero = jnp.zeros((8, D), F32)
        for r, val in enumerate(lax.fori_loop(0, 8, sum_strip, (zero, zero), unroll=2)):
            val = jnp.sum(val, axis=0, keepdims=True)
            for n in range(4):
                R["ln"][0, 4 * r + n : 4 * r + n + 1, :] = val[:, n * 256 : (n + 1) * 256]

    def last_strip(u, carry):
        ru = pl.ds(pl.multiple_of(u * 32, 32), 32)
        r = pl.ds(pl.multiple_of(mine_at + u * 32, 32), 32)
        xin = tokens[ru, :].astype(F32)
        total = outp[r, :] + rxs[0, ru, :].astype(F32)
        o_out[ru, :] = (xin + total + vecs[2:3, :] + vecs[3:4, :]).astype(BF)
        rs = mr[1, ru, 0:1]
        hat = (xin - mr[0, ru, 0:1]) * rs
        n = gnp[r, :] * gain
        grad = n - jnp.mean(n, axis=-1, keepdims=True) - hat * jnp.mean(n * hat, axis=-1, keepdims=True)
        o_tok[ru, :] = cot[ru, :].astype(F32) + grad * rs
        return carry

    own_heads = (xo, yh * 512, 0, (0, 1))

    tables_()
    loaded(0, 2)
    grad_mixed(at256(own))
    loaded(2, 2)
    loop(2, lambda i: tile(0, i, c * 256, 256))
    cot_s.wait_recv()
    grad_mixed(at256(sib))
    send_grad_mixed()
    cot_p.start()
    nrm_s.wait_recv()
    loop(2, lambda i: tile(0, i, (1 - c) * 256, 256))
    grads_in(0, 0)
    red_a = reduce_in(0, 0, 512)
    red_a.step()
    tiles(0, 1)
    grads_in(0, 1)
    red_b = reduce_in(0, 512, 512)
    red_b.step()
    grads_down(0)
    red_a.step()
    red_c = reduce_down(0)
    red_c.step()
    tiles(1, 0)
    red_b.step()
    tiles(1, 1)
    grads_in(1, 0)
    grads_in(1, 1)
    red_a.step()
    red_d = reduce_in(1, 0, 1024)
    red_d.step()
    grads_down(1)
    red_c.step()
    red_e = reduce_down(1)
    red_e.step()
    loaded(10, 12)
    qkv_block(own)
    qkv_block(sib)
    nrm_p.wait_recv()
    nrm_f = forward(nal)
    for cp in back_do:
        cp.wait_send()
    qkv_block(par)
    nrm_f.wait_recv()
    qkv_block(dia)
    for cp in back_do:
        cp.wait_recv()
    red_b.step()
    attend(0, 3)
    red_a.step()
    attend(0, 2)
    red_d.step()
    attend(0, 1)
    attend(0, 0)
    send_back(0)
    qkv_grads(0)
    red2 = reduce_qkv(0)
    red2.step()
    attend(1, 3)
    red_c.step()
    attend(1, 2)
    attend(1, 1)
    attend(1, 0)
    send_back(1)
    red_e.step()
    qkv_grads(1)
    red3 = reduce_qkv(1)
    red3.step()
    red2.step()
    cot_p.wait_recv()
    cot_f = forward(cal)
    for g in range(2):
        bias_grads(g)
    sums = exchange(0, 0, early, plane_devices)
    cot_f.wait_recv()
    for g in range(2):
        out_grads(g)
    red4 = reduce_out()
    red4.step()
    loop(2, ffn_out)
    red_d.step()
    red_a.step()
    red_b.step()
    loop(2, lambda n: ffn_out(n + 2))
    red_c.step()
    red3.step()
    red4.step()
    red2.step()
    plane_sum(early, sums)
    sums = exchange(1, 15, early, pairs_y)
    project(*own_heads, theirs_at)
    red_e.step()
    red_a.step()
    red_b.step()
    back[0].wait_recv()
    project(xr, 0, 1, (0,), theirs_at)
    red_d.step()
    red_c.step()
    project(*own_heads, mine_at)
    red3.step()
    red4.step()
    project(xr, 0, 1, (0,), mine_at)
    red_e.step()
    red_d.step()
    red2.step()
    red_b.step()
    red_c.step()
    finish_sums(early, sums, o_small)
    back[1].wait_recv()
    project(xr, 0, 1, (1,), theirs_at)
    loop(4, stage_strip)
    swap = [Pieces(links, stage.at[pl.ds(w * 256, 256), :], rxs.at[w], sibling, PIECE) for w in range(2)]
    for cp in swap:
        cp.start()
    project(xr, 0, 1, (1,), mine_at)
    red_e.step()
    red3.step()
    red_d.step()
    for cp in swap:
        cp.wait()
    norm_sums()
    sums = exchange(0, 0, late, plane_devices)
    lax.fori_loop(0, 8, last_strip, 0, unroll=2)
    red4.step()
    red_e.step()
    plane_sum(late, sums)
    sums = exchange(1, 15, late, pairs_y)
    for cp in (cot_s, nrm_s, cot_p, nrm_p, cot_f, nrm_f):
        cp.wait_send()
    finish_sums(late, sums, o_ln)
    for cp in back:
        cp.wait_send()
    for cp, sends, arrives in finals:
        if sends is None:
            cp.wait()
        else:
            pl.when(sends)(cp.wait_send)
            pl.when(arrives)(cp.wait_recv)
    assert [r.at for r in (red_a, red_b, red_c, red_d, red_e)] == [6] * 5
    assert [r.at for r in (red2, red3, red4)] == [4] * 3
    assert links.count <= NSEM, links.count


def hand_over(*refs):
    raw, small, ln = refs[:6], refs[6], refs[7]
    outs, vec, line = refs[8:14], refs[14:20], refs[20]
    for src, dst in zip(raw, outs):
        dst[...] = src[...]
    index = lax.axis_index("dp") * 4 + lax.axis_index("seq")
    for r in (3, 5):
        line[r : r + 1, 0:D] = small[0, 4:5, :] + small[1, 4:5, :]
    for r in range(2):
        for n in range(4):
            row = slice(4 * r + n, 4 * r + n + 1)
            line[r : r + 1, n * 256 : (n + 1) * 256] = ln[0, row, :] + ln[1, row, :]
    for t in range(4):
        line[4:5, t * 1024 : (t + 1) * 1024] = small[t % 2, t // 2 : t // 2 + 1, :]
        for j in range(3):
            line[2:3, pl.ds(j * 1024 + t * 256, 256)] = small[t % 2, 2 + t // 2 : 3 + t // 2, j * 256 : (j + 1) * 256]
    for r, out in enumerate(vec):
        n = out.shape[0]
        at = index * n
        part = line[r : r + 1, pl.ds(pl.multiple_of((at // 128) * 128, 128), 256)]
        part = pltpu.roll(jnp.broadcast_to(part, (8, 256)), (256 - at % 128) % 256, 1)
        out[...] = part[0, 0:n]


def on_device(tokens, lengths, ln_gain, ln_bias, w_qkv, b_qkv, w_out, b_out, w_in, b_in, w_down, b_down, cotangent):
    V = pl.BlockSpec(memory_space=pltpu.VMEM)
    H = pl.BlockSpec(memory_space=pl.ANY)
    S = pl.BlockSpec(memory_space=pltpu.SMEM)
    sds = jax.ShapeDtypeStruct
    outs = pl.pallas_call(
        kernel,
        out_shape=[
            sds((BLK, D), BF),
            sds((BLK, D), F32),
            sds((8, 3 * D), F32),
            sds((8, D), F32),
            sds((8, 4 * D), F32),
            sds((32, D), F32),
            sds((2, 8, 1024), F32),
            sds((2, 8, 256), F32),
        ],
        in_specs=[V] * 6 + [S, V, V, H, H, H, H],
        out_specs=[V] * 8,
        scratch_shapes=[pltpu.VMEM(shape, dt) for _, shape, dt in SCRATCH]
        + [pltpu.SemaphoreType.DMA((NSEM,)), pltpu.SemaphoreType.DMA((NSEM,)), pltpu.SemaphoreType.DMA((NLOC,))],
        compiler_params=pltpu.CompilerParams(collective_id=0, has_side_effects=True, vmem_limit_bytes=VMEM_LIMIT),
        name="layer",
    )(ln_gain, ln_bias, b_out, b_down, b_qkv, b_in, lengths, tokens[0], cotangent[0], w_qkv, w_out, w_in, w_down)
    vec = [sds((n // 128,), F32) for n in (D, D, 3 * D, D, 4 * D, D)]
    finals = pl.pallas_call(
        hand_over,
        out_shape=[sds(o.shape, o.dtype) for o in outs[:6]] + vec,
        in_specs=[V] * 8,
        out_specs=[V] * 12,
        scratch_shapes=[pltpu.VMEM((8, 4 * D + 128), F32)],
        name="shares",
    )(*outs)
    out, grad_tokens, g_wqkv, g_wout, g_win, g_wdn, g_gain, g_bias, g_bqkv, g_bout, g_bin, g_bdown = finals
    return (out[None], grad_tokens[None], g_gain, g_bias, g_wqkv, g_bqkv, g_wout, g_bout, g_win, g_bin, g_wdn, g_bdown)


def solution(mesh):
    act, vec, mat = P("dp", "seq", None), P(("dp", "seq")), P(("dp", "seq"), None)
    return jax.shard_map(
        on_device,
        mesh=mesh,
        in_specs=(act, P("dp", None)) + (P(),) * 10 + (act,),
        out_specs=(act, act, vec, vec, mat, vec, mat, vec, mat, vec, mat, vec),
        check_vma=False,
    )
```

time: 121 us -> 106 us (0.88)
  Pallas kernels: 119 us -> 105 us
    pallas_call x1, Pallas kernels: 116 us -> 102 us  [on_device(): pl.pallas_call(kernel, out_shape=[sds((BLK, D), BF), sds((BLK, D), F32),...]
where the time goes in v3:
time: 106 us
  Pallas kernels  105 us (99%)
    pallas_call x1, Pallas kernels, on_device(): pl.pallas_call(kernel, out_shape=[sds((BLK, D), BF), sds((BLK, D), F32),...  102 us
    pallas_call x1, Pallas kernels, on_device(): pl.pallas_call(hand_over, out_shape=[sds(o.shape, o.dtype) for o in outs[...  2.89 us

profile of v3, /device:TPU:1, one launch (start us, length us, event | category | flops | bytes accessed | tf_op | source)
XLA Modules:
  0.0 106.2 jit_solution(5080040927092254942)
XLA Ops:
  0.6 102.5 %layer.1 = (bf16[256,1024]{1,0:T(8,128)(2,1)}, f32[256,1024]{1,0:T(8,128)}, f32[8,3072]{1,0:T(8,128)}, f32[8,1024]{1,0:T(8,128)}, f32[8,4096]{1,0:T(8,128)}, /*i...) custom-call(bf16[1024]{0:T(1024)(128)(2,1)} %refs_0_.1, bf16[1024]{0:T(1024)(128)(2,1)} %refs_1_.1, ...), custom_call_target="tpu_custom_call" | custom-call | tf_op jit(solution)/shard_map/layer/pallas_call | solution.py:981
  103.1 2.9 %shares.1 = (bf16[256,1024]{1,0:T(8,128)(2,1)}, f32[256,1024]{1,0:T(8,128)}, f32[8,3072]{1,0:T(8,128)}, f32[8,1024]{1,0:T(8,128)}, f32[8,4096]{1,0:T(8,128)}, /*...) custom-call(bf16[256,1024]{1,0:T(8,128)(2,1)} %get-tuple-element.32., ...), custom_call_target="tpu_custom_call" | custom-call | tf_op jit(solution)/shard_map/shares/pallas_call | solution.py:1001

commit v4 on v3

--- a/solution.py
+++ b/solution.py
@@ -91,41 +91,53 @@
     ("fin_out", (16, 512), F32),
 ]
 PIECE = 32
-NSEM = 384
-NLOC = 24
+NSEND = 63
+NRECV = 89
+NLOC = 10
 
 
 class Links:
-    def __init__(self, send, recv):
-        self.send, self.recv, self.count = send, recv, 0
-
-    def copy(self, src, dst, device):
-        k = self.count
-        self.count += 1
+    def __init__(self, send, recv, away):
+        self.send, self.recv, self.away = send, recv, away
+        self.sends = self.recvs = 0
+
+    def new_send(self):
+        self.sends += 1
+        return self.send.at[self.sends - 1]
+
+    def new_recv(self):
+        self.recvs += 1
+        return self.recv.at[self.recvs - 1]
+
+    def copy(self, src, dst, device, send=None, recv=None):
         return pltpu.make_async_remote_copy(
             src_ref=src,
             dst_ref=dst,
-            send_sem=self.send.at[k],
-            recv_sem=self.recv.at[k],
+            send_sem=self.new_send() if send is None else send,
+            recv_sem=self.new_recv() if recv is None else recv,
             device_id=device,
             device_id_type=MESH,
         )
 
-
-class Pieces:
-    def __init__(self, links, src, dst, device, rows):
-        self.whole = links.copy(src, dst, device)
-        k = links.count - 1
-        self.parts = []
-        for at in range(0, src.shape[0], rows):
-            part = pl.ds(at, rows)
-            links.count = k
-            self.parts.append(links.copy(src.at[part], dst.at[part], device))
-        self.wait, self.wait_send, self.wait_recv = self.whole.wait, self.whole.wait_send, self.whole.wait_recv
+    def whole(self, view, send, recv):
+        return self.copy(view, view, self.away, send, recv)
+
+
+class Group:
+    def __init__(self, links, view, copies):
+        send, recv = links.new_send(), links.new_recv()
+        self.parts = [links.copy(src, dst, d, send, recv) for src, dst, d in copies]
+        whole = links.whole(view, send, recv)
+        self.wait, self.wait_send, self.wait_recv = whole.wait, whole.wait_send, whole.wait_recv
 
     def start(self):
         for cp in self.parts:
             cp.start()
+
+
+def pieces(links, src, dst, device, rows):
+    cuts = [pl.ds(at, rows) for at in range(0, src.shape[0], rows)]
+    return Group(links, src, [(src.at[p], dst.at[p], device) for p in cuts])
 
 
 def add_into(dst, sources):
@@ -144,37 +156,33 @@
         self.block, self.land = block, land
         self.pos = pos
         self.rt, self.lf, self.opp = (pos + 1) % 4, (pos + 3) % 4, (pos + 2) % 4
-        c = links.copy
-        self.early = [
-            c(block(self.opp, 0), land.at[0], right),
-            c(block(self.opp, 1), land.at[1], left),
-            c(block(self.rt, 1), land.at[2], right),
-            c(block(self.lf, 0), land.at[3], left),
-        ]
-        self.late = [
-            c(block(self.rt, 0), land.at[4], right),
-            c(block(self.lf, 1), land.at[5], left),
-        ]
+        send, near, far = links.new_send(), links.new_recv(), links.new_recv()
+
+        def c(t, half, slot, device):
+            return links.copy(block(t, half), land.at[slot], device, send, near if slot < 2 else far)
+
+        self.early = [c(self.opp, 0, 0, right), c(self.opp, 1, 1, left), c(self.rt, 1, 2, right), c(self.lf, 0, 3, left)]
+        self.late = [c(self.rt, 0, 4, right), c(self.lf, 1, 5, left)]
+        self.near = links.whole(land.at[pl.ds(0, 2)], send, near)
+        self.far = links.whole(land.at[pl.ds(2, 4)], send, far)
+        self.sent = links.whole(land, send, far)
 
     def start(self):
         for c in self.early:
             c.start()
 
     def middle(self):
-        self.early[0].wait_recv()
+        self.near.wait_recv()
         add_into(self.block(self.rt, 0), [self.land.at[0]])
         self.late[0].start()
-        self.early[1].wait_recv()
         add_into(self.block(self.lf, 1), [self.land.at[1]])
         self.late[1].start()
 
     def finish(self):
-        for c in self.early[2:] + self.late:
-            c.wait_recv()
+        self.far.wait_recv()
         add_into(self.block(self.pos, 0), [self.land.at[4], self.land.at[3]])
         add_into(self.block(self.pos, 1), [self.land.at[2], self.land.at[5]])
-        for c in self.early + self.late:
-            c.wait_send()
+        self.sent.wait_send()
 
 
 class Reduce:
@@ -198,7 +206,7 @@
         ]
         both = pl.ds(col, width)
         self.own = ref.at[x, y, z, every, both]
-        self.last = [links.copy(ref.at[x, ty, z, every, both], self.land_y.at[n], d) for n, (ty, d) in enumerate(last)]
+        self.last = Group(links, self.land_y, [(ref.at[x, ty, z, every, both], self.land_y.at[n], d) for n, (ty, d) in enumerate(last)])
         self.after = after
         self.at = 0
 
@@ -227,11 +235,9 @@
         elif self.at == 4:
             for r in two:
                 r.finish()
-            for cp in self.last:
-                cp.start()
+            self.last.start()
         elif self.at == 5:
-            for cp in self.last:
-                cp.wait()
+            self.last.wait()
             self.after(self)
         self.at += 1
 
@@ -249,8 +255,8 @@
         self.own = [ref.at[x, yl, z, :, c] for c in cols]
         self.lands = (land2z, land2x)
         self.two = [
-            [links.copy(ref.at[tx, ty, z, :, cols[0]], land2z.at[n], d) for n, (tx, ty, d) in enumerate(far[0])],
-            [links.copy(ref.at[x, ty, tz, :, cols[1]], land2x.at[n], d) for n, (tz, ty, d) in enumerate(far[1])],
+            Group(links, land2z, [(ref.at[tx, ty, z, :, cols[0]], land2z.at[n], d) for n, (tx, ty, d) in enumerate(far[0])]),
+            Group(links, land2x, [(ref.at[x, ty, tz, :, cols[1]], land2x.at[n], d) for n, (tz, ty, d) in enumerate(far[1])]),
         ]
         self.cols, self.after, self.at = cols, after, 0
 
@@ -264,12 +270,10 @@
         elif self.at == 2:
             for r, cps in zip(self.one, self.two):
                 r.finish()
-                for cp in cps:
-                    cp.start()
+                cps.start()
         elif self.at == 3:
             for cps in self.two:
-                for cp in cps:
-                    cp.wait()
+                cps.wait()
             self.after(self)
         self.at += 1
 
@@ -287,7 +291,6 @@
     rest = refs[21:]
     R = {name: r for (name, _, _), r in zip(SCRATCH, rest)}
     send, recv, loc = rest[len(SCRATCH) :]
-    links = Links(send, recv)
 
     dpi, s = lax.axis_index("dp"), lax.axis_index("seq")
     z, x, yl = dpi // 8, (dpi // 2) % 4, dpi % 2
@@ -310,6 +313,7 @@
     partner = dev(z, x, y + 2, c)
     diagonal = dev(z, x, y + 2, 1 - c)
 
+    links = Links(send, recv, sibling)
     meet = [at_x(d) for d in (1, 2, 3)] + [at_y(d) for d in (1, 2, 3)] + [sibling, diagonal]
     for d in (1, 2, 3):
         for cc in (c, 1 - c):
@@ -325,23 +329,27 @@
 
     loads = []
 
-    def load(src, dst):
-        cp = pltpu.make_async_copy(src, dst, loc.at[len(loads)])
+    def load(src, dst, n):
+        cp = pltpu.make_async_copy(src, dst, loc.at[n])
         cp.start()
-        loads.append(cp)
-
-    for w, sw in enumerate((s, (1 - yh) * 2 + c)):
-        load(w_out.at[at256(sw), :], R["wout"].at[w])
+        return cp
+
+    heads_of = (s, (1 - yh) * 2 + c)
+    for w, sw in enumerate(heads_of):
+        load(w_out.at[at256(sw), :], R["wout"].at[w], 0)
+    loads.append(pltpu.make_async_copy(R["wout"], R["wout"], loc.at[0]))
     for a in range(2):
         for h in range(2):
+            n = 1 + 4 * a + 2 * h
             wide = pl.ds(pl.multiple_of((2 * a + c) * 1024 + h * 512, 512), 512)
-            load(w_in.at[:, wide], R["win"].at[a, :, pl.ds(h * 512, 512)])
-            load(w_down.at[wide, :], R["wdn"].at[a, pl.ds(h * 512, 512), :])
-    for w, sw in enumerate((s, (1 - yh) * 2 + c)):
+            loads.append(load(w_in.at[:, wide], R["win"].at[a, :, pl.ds(h * 512, 512)], n))
+            loads.append(load(w_down.at[wide, :], R["wdn"].at[a, pl.ds(h * 512, 512), :], n + 1))
+    for w, sw in enumerate(heads_of):
         for g in range(2):
             for j in range(3):
                 cols = pl.ds(pl.multiple_of(j * 1024 + sw * 256 + g * 128, 128), 128)
-                load(w_qkv.at[:, cols], R["wqkv"].at[w, g, :, pl.ds(j * 128, 128)])
+                load(w_qkv.at[:, cols], R["wqkv"].at[w, g, :, pl.ds(j * 128, 128)], 9)
+    loads.append(pltpu.make_async_copy(R["wqkv"], R["wqkv"], loc.at[9]))
 
     def loaded(first, count):
         for cp in loads[first : first + count]:
@@ -350,7 +358,7 @@
     own, sib = s, yh * 2 + 1 - c
     par, dia = (1 - yh) * 2 + c, (1 - yh) * 2 + 1 - c
     cal, nal = R["call"], R["nall"]
-    cot_s = Pieces(links, cot, cal.at[at256(own), :], sibling, PIECE)
+    cot_s = pieces(links, cot, cal.at[at256(own), :], sibling, PIECE)
     cot_p = links.copy(cot, cal.at[at256(own), :], partner)
     cal[at256(own), :] = cot[...]
 
@@ -375,7 +383,7 @@
 
     lax.fori_loop(0, 8, norm_strip, 0, unroll=2)
     mine = nal.at[at256(own), :]
-    nrm_s = Pieces(links, mine, mine, sibling, PIECE)
+    nrm_s = pieces(links, mine, mine, sibling, PIECE)
     nrm_p = links.copy(mine, mine, partner)
     pl.semaphore_wait(barrier, len(meet))
     for cp in (cot_s, nrm_s, nrm_p):
@@ -468,17 +476,17 @@
         sm[0, a : a + 1, cs] += jnp.sum(total, axis=0, keepdims=True)
 
     def tiles(a, h):
-        loaded(2 + 4 * a + 2 * h, 2)
+        loaded(1 + 4 * a + 2 * h, 2)
         loop(2, lambda i: tile(a, 2 * h + i, 0, 512))
 
     g_ffn = R["g_ffn"]
 
-    def grads_in(a, h):
+    def grads_in(a, col, width):
         half = pl.ds(a * 512, 512)
 
         def part(m):
-            res = dot_tn(nal[here, at256(m)], gh[half, pl.ds(h * 512, 512)]).astype(BF)
-            g_ffn[a, 0, :, :, m, :, pl.ds(h * 512, 512)] = res.reshape(4, 4, 16, 512)
+            res = dot_tn(nal[here, at256(m)], gh[half, pl.ds(col, width)]).astype(BF)
+            g_ffn[a, 0, :, :, m, :, pl.ds(col, width)] = res.reshape(4, 4, 16, width)
 
         loop(4, part)
 
@@ -491,21 +499,14 @@
 
         loop(4, part)
 
-    def ffn_out(n):
-        cs = at256(n)
-        top, low = pl.ds(0, 512), pl.ds(512, 512)
-        outp[:, cs] = dot_nn(act[top, :], wdn[0, :, cs]) + dot_nn(act[low, :], wdn[1, :, cs])
-        gnp[:, cs] = dot_nt(gh[top, :], win[0, cs, :]) + dot_nt(gh[low, :], win[1, cs, :])
-
     finals = []
 
-    def put(src, dst, device, sends=None, arrives=None):
+    shared = [(links.new_send(), links.new_recv()) for _ in range(2)]
+
+    def put(src, dst, device, sends, arrives):
         cp = links.copy(src, dst, device)
         finals.append((cp, sends, arrives))
-        if sends is None:
-            cp.start()
-        else:
-            pl.when(sends)(cp.start)
+        pl.when(sends)(cp.start)
 
     def keep(src, dst, here_too):
         @pl.when(here_too)
@@ -519,7 +520,7 @@
             cols = pl.ds(pl.multiple_of((2 * a + c) * 1024 + col, 512), width)
             fin = fin_ffn.at[a, 0, :, pl.ds(col, width)]
             red.result_into(fin)
-            put(fin.at[pl.ds(pl.multiple_of((1 - c) * 8, 8), 8), :], o_win.at[:, cols], sibling)
+            links.copy(fin.at[pl.ds(pl.multiple_of((1 - c) * 8, 8), 8), :], o_win.at[:, cols], sibling, *shared[0]).start()
             o_win[:, cols] = fin[pl.ds(pl.multiple_of(c * 8, 8), 8), :]
 
         return done
@@ -547,7 +548,8 @@
                 dst_l = pl.ds(pl.multiple_of(j * 1024 + s * 256 + g * 128, 128), 128)
                 for d in (1, 2, 3):
                     t = (s + d) % 4
-                    put(fin_qkv.at[g, pl.ds(pl.multiple_of(t * 8, 8), 8), src_l], o_wqkv.at[:, dst_l], (dpi, t))
+                    src = fin_qkv.at[g, pl.ds(pl.multiple_of(t * 8, 8), 8), src_l]
+                    links.copy(src, o_wqkv.at[:, dst_l], (dpi, t), *shared[1]).start()
                 o_wqkv[:, dst_l] = fin_qkv[g, pl.ds(pl.multiple_of(s * 8, 8), 8), src_l]
 
         return done
@@ -713,17 +715,23 @@
 
     mine_at, theirs_at = c * 256, (1 - c) * 256
 
-    def project(src, base, w, pairs, at):
-        dst = pl.ds(pl.multiple_of(at, 256), 256)
-        rows = pl.ds(pl.multiple_of(base + at, 256), 256)
+    def outputs(n):
+        cs = at256(n)
+        top, low, every = pl.ds(0, 512), pl.ds(512, 512), pl.ds(0, 512)
+        o = dot_nn(act[top, :], wdn[0, :, cs]) + dot_nn(act[low, :], wdn[1, :, cs])
+        g = dot_nt(gh[top, :], win[0, cs, :]) + dot_nt(gh[low, :], win[1, cs, :])
+        for src, rows, w, p in ((xo, here, 0, 0), (xo, here, 0, 1), (xr, every, 1, 0)):
+            o += dot_nn(src[rows, pl.ds(p * 512 + 384, 128)], wout[w, pl.ds(p * 128, 128), cs])
+            g += dot_nt(src[rows, pl.ds(p * 512, 384)], wqkv[w, p, cs, :])
+        outp[:, cs], gnp[:, cs] = o, g
+
+    def project_last(at):
+        rows = pl.ds(pl.multiple_of(at, 256), 256)
 
         def part(n):
             cs = at256(n)
-            add_o, add_g = outp[dst, cs], gnp[dst, cs]
-            for g in pairs:
-                add_o += dot_nn(src[rows, pl.ds(g * 512 + 384, 128)], wout[w, pl.ds(g * 128, 128), cs])
-                add_g += dot_nt(src[rows, pl.ds(g * 512, 384)], wqkv[w, g, cs, :])
-            outp[dst, cs], gnp[dst, cs] = add_o, add_g
+            outp[rows, cs] += dot_nn(xr[rows, pl.ds(896, 128)], wout[1, pl.ds(128, 128), cs])
+            gnp[rows, cs] += dot_nt(xr[rows, pl.ds(512, 384)], wqkv[1, 1, cs, :])
 
         loop(4, part)
 
@@ -740,22 +748,20 @@
     early, late = (sm, smr), (R["ln"], R["lnr"])
 
     def exchange(level, slot, bufs, devices):
-        cps = [links.copy(bufs[0].at[level], bufs[1].at[slot + d], t) for d, t in enumerate(devices)]
-        for cp in cps:
-            cp.start()
+        view = bufs[1].at[pl.ds(slot, len(devices))]
+        cps = Group(links, view, [(bufs[0].at[level], bufs[1].at[slot + d], t) for d, t in enumerate(devices)])
+        cps.start()
         return cps
 
     def plane_sum(bufs, cps):
-        for cp in cps:
-            cp.wait()
+        cps.wait()
         total = bufs[0][0]
-        for d in range(len(cps)):
+        for d in range(15):
             total = total + bufs[1][d]
         bufs[0][1] = total
 
     def finish_sums(bufs, cps, out):
-        for cp in cps:
-            cp.wait()
+        cps.wait()
         same, other = bufs[0][1], bufs[1][18]
         for d in range(3):
             same = same + bufs[1][15 + d]
@@ -772,7 +778,7 @@
 
     def forward(buf):
         rows = buf.at[at256(par), :]
-        cp = Pieces(links, rows, rows, sibling, PIECE)
+        cp = pieces(links, rows, rows, sibling, PIECE)
         cp.start()
         return cp
 
@@ -805,12 +811,10 @@
         o_tok[ru, :] = cot[ru, :].astype(F32) + grad * rs
         return carry
 
-    own_heads = (xo, yh * 512, 0, (0, 1))
-
     tables_()
-    loaded(0, 2)
+    loaded(0, 1)
     grad_mixed(at256(own))
-    loaded(2, 2)
+    loaded(1, 2)
     loop(2, lambda i: tile(0, i, c * 256, 256))
     cot_s.wait_recv()
     grad_mixed(at256(sib))
@@ -818,11 +822,11 @@
     cot_p.start()
     nrm_s.wait_recv()
     loop(2, lambda i: tile(0, i, (1 - c) * 256, 256))
-    grads_in(0, 0)
+    grads_in(0, 0, 512)
     red_a = reduce_in(0, 0, 512)
     red_a.step()
     tiles(0, 1)
-    grads_in(0, 1)
+    grads_in(0, 512, 512)
     red_b = reduce_in(0, 512, 512)
     red_b.step()
     grads_down(0)
@@ -832,8 +836,7 @@
     tiles(1, 0)
     red_b.step()
     tiles(1, 1)
-    grads_in(1, 0)
-    grads_in(1, 1)
+    grads_in(1, 0, 1024)
     red_a.step()
     red_d = reduce_in(1, 0, 1024)
     red_d.step()
@@ -841,7 +844,7 @@
     red_c.step()
     red_e = reduce_down(1)
     red_e.step()
-    loaded(10, 12)
+    loaded(9, 1)
     qkv_block(own)
     qkv_block(sib)
     nrm_p.wait_recv()
@@ -885,29 +888,25 @@
         out_grads(g)
     red4 = reduce_out()
     red4.step()
-    loop(2, ffn_out)
     red_d.step()
     red_a.step()
     red_b.step()
-    loop(2, lambda n: ffn_out(n + 2))
+    back[0].wait_recv()
+    loop(2, outputs)
     red_c.step()
     red3.step()
     red4.step()
     red2.step()
     plane_sum(early, sums)
     sums = exchange(1, 15, early, pairs_y)
-    project(*own_heads, theirs_at)
     red_e.step()
     red_a.step()
     red_b.step()
-    back[0].wait_recv()
-    project(xr, 0, 1, (0,), theirs_at)
+    loop(2, lambda n: outputs(n + 2))
     red_d.step()
     red_c.step()
-    project(*own_heads, mine_at)
     red3.step()
     red4.step()
-    project(xr, 0, 1, (0,), mine_at)
     red_e.step()
     red_d.step()
     red2.step()
@@ -915,12 +914,12 @@
     red_c.step()
     finish_sums(early, sums, o_small)
     back[1].wait_recv()
-    project(xr, 0, 1, (1,), theirs_at)
+    project_last(theirs_at)
     loop(4, stage_strip)
-    swap = [Pieces(links, stage.at[pl.ds(w * 256, 256), :], rxs.at[w], sibling, PIECE) for w in range(2)]
+    swap = [pieces(links, stage.at[pl.ds(w * 256, 256), :], rxs.at[w], sibling, PIECE) for w in range(2)]
     for cp in swap:
         cp.start()
-    project(xr, 0, 1, (1,), mine_at)
+    project_last(mine_at)
     red_e.step()
     red3.step()
     red_d.step()
@@ -938,15 +937,14 @@
     finish_sums(late, sums, o_ln)
     for cp in back:
         cp.wait_send()
+    links.whole(o_win.at[:, pl.ds(0, 2048)], *shared[0]).wait()
+    links.whole(o_wqkv.at[:, pl.ds(0, 2304)], *shared[1]).wait()
     for cp, sends, arrives in finals:
-        if sends is None:
-            cp.wait()
-        else:
-            pl.when(sends)(cp.wait_send)
-            pl.when(arrives)(cp.wait_recv)
+        pl.when(sends)(cp.wait_send)
+        pl.when(arrives)(cp.wait_recv)
     assert [r.at for r in (red_a, red_b, red_c, red_d, red_e)] == [6] * 5
     assert [r.at for r in (red2, red3, red4)] == [4] * 3
-    assert links.count <= NSEM, links.count
+    assert (links.sends, links.recvs) == (NSEND, NRECV), (links.sends, links.recvs)
 
 
 def hand_over(*refs):
@@ -993,7 +991,7 @@
         in_specs=[V] * 6 + [S, V, V, H, H, H, H],
         out_specs=[V] * 8,
         scratch_shapes=[pltpu.VMEM(shape, dt) for _, shape, dt in SCRATCH]
-        + [pltpu.SemaphoreType.DMA((NSEM,)), pltpu.SemaphoreType.DMA((NSEM,)), pltpu.SemaphoreType.DMA((NLOC,))],
+        + [pltpu.SemaphoreType.DMA((NSEND,)), pltpu.SemaphoreType.DMA((NRECV,)), pltpu.SemaphoreType.DMA((NLOC,))],
         compiler_params=pltpu.CompilerParams(collective_id=0, has_side_effects=True, vmem_limit_bytes=VMEM_LIMIT),
         name="layer",
     )(ln_gain, ln_bias, b_out, b_down, b_qkv, b_in, lengths, tokens[0], cotangent[0], w_qkv, w_out, w_in, w_down)

time: 106 us -> 102 us (0.962)
  Pallas kernels: 105 us -> 101 us
    pallas_call x1, Pallas kernels: 102 us -> 98.1 us  [on_device(): pl.pallas_call(kernel, out_shape=[sds((BLK, D), BF), sds((BLK, D), F32),...]
where the time goes in v4:
time: 102 us
  Pallas kernels  101 us (99%)
    pallas_call x1, Pallas kernels, on_device(): pl.pallas_call(kernel, out_shape=[sds((BLK, D), BF), sds((BLK, D), F32),...  98.1 us
    pallas_call x1, Pallas kernels, on_device(): pl.pallas_call(hand_over, out_shape=[sds(o.shape, o.dtype) for o in outs[...  2.89 us

profile of v4, /device:TPU:1, one launch (start us, length us, event | category | flops | bytes accessed | tf_op | source)
XLA Modules:
  0.0 101.9 jit_solution(9926306457232842533)
XLA Ops:
  0.6 98.1 %layer.1 = (bf16[256,1024]{1,0:T(8,128)(2,1)}, f32[256,1024]{1,0:T(8,128)}, f32[8,3072]{1,0:T(8,128)}, f32[8,1024]{1,0:T(8,128)}, f32[8,4096]{1,0:T(8,128)}, /*i...) custom-call(bf16[1024]{0:T(1024)(128)(2,1)} %refs_0_.1, bf16[1024]{0:T(1024)(128)(2,1)} %refs_1_.1, ...), custom_call_target="tpu_custom_call" | custom-call | tf_op jit(solution)/shard_map/layer/pallas_call | solution.py:979
  98.8 2.9 %shares.1 = (bf16[256,1024]{1,0:T(8,128)(2,1)}, f32[256,1024]{1,0:T(8,128)}, f32[8,3072]{1,0:T(8,128)}, f32[8,1024]{1,0:T(8,128)}, f32[8,4096]{1,0:T(8,128)}, /*...) custom-call(bf16[256,1024]{1,0:T(8,128)(2,1)} %get-tuple-element.32., ...), custom_call_target="tpu_custom_call" | custom-call | tf_op jit(solution)/shard_map/shares/pallas_call | solution.py:999

commit v5 on v4

--- a/solution.py
+++ b/solution.py
@@ -71,10 +71,17 @@
     ("xr", (512, 1024), BF),
     ("tab", (2, ROW, 128), F32),
     ("mr", (2, BLK, 128), F32),
-    ("sm", (2, 8, 1024), F32),
-    ("smr", (22, 8, 1024), F32),
-    ("ln", (2, 8, 256), F32),
-    ("lnr", (22, 8, 256), F32),
+    ("sm", (1, 8, 1024), F32),
+    ("sp", (1, 16, 256), BF),
+    ("spr", (15, 16, 256), BF),
+    ("sq", (1, 16, 256), F32),
+    ("sqr", (7, 16, 256), F32),
+    ("ln", (16, 1, 128), F32),
+    ("lnr", (15, 1, 128), F32),
+    ("lnp", (1, 1, 128), F32),
+    ("lnq", (7, 1, 128), F32),
+    ("tsib", (BLK, D), BF),
+    ("msib", (2, BLK, 128), F32),
     ("rxs", (2, BLK, D), BF),
     ("r1z_ffn", (2, 6, 2, 4, 2, 16, 512), BF),
     ("r1x_ffn", (2, 6, 2, 2, 4, 16, 512), BF),
@@ -91,8 +98,8 @@
     ("fin_out", (16, 512), F32),
 ]
 PIECE = 32
-NSEND = 63
-NRECV = 89
+NSEND = 65
+NRECV = 91
 NLOC = 10
 
 
@@ -386,10 +393,12 @@
     nrm_s = pieces(links, mine, mine, sibling, PIECE)
     nrm_p = links.copy(mine, mine, partner)
     pl.semaphore_wait(barrier, len(meet))
-    for cp in (cot_s, nrm_s, nrm_p):
+    tok_s = pieces(links, tokens, R["tsib"], sibling, PIECE)
+    sta_s = links.copy(mr, R["msib"], sibling)
+    for cp in (cot_s, nrm_s, nrm_p, tok_s, sta_s):
         cp.start()
 
-    sm, smr = R["sm"], R["smr"]
+    sm = R["sm"]
     sm[0] = jnp.zeros((8, 1024), F32)
     sm[0, 4:5, :] = jnp.sum(cot[...].astype(F32), axis=0, keepdims=True)
 
@@ -681,11 +690,17 @@
 
     back = []
 
-    def send_back(g):
+    def start_back(g):
         cols = pl.ds(g * 512, 512)
-        cp = links.copy(xo.at[there, cols], xr.at[:, cols], partner)
-        cp.start()
-        back.append(cp)
+        view = xr.at[:, cols]
+        copies = [(xo.at[pl.ds(256 * i, 256), cols], xr.at[pl.ds(256 * (i % 2), 256), cols], partner) for i in range(4)]
+        back.append(Group(links, view, copies))
+
+    def send_back(g, i):
+        pl.when(yh != i // 2)(back[g].parts[i].start)
+
+    start_back(0)
+    start_back(1)
 
     def qkv_grads(g):
         def part(m):
@@ -703,9 +718,7 @@
 
         total = jnp.sum(lax.fori_loop(0, 16, part, total), axis=0, keepdims=True)
         for j in range(3):
-            for h in range(2):
-                val = jnp.where(yh == h, total[:, j * 128 : (j + 1) * 128], 0.0)
-                sm[0, 2 + h : 3 + h, pl.ds(j * 256 + g * 128, 128)] = val
+            sm[0, 2:3, pl.ds(j * 256 + g * 128, 128)] = total[:, j * 128 : (j + 1) * 128]
 
     def out_grads(g):
         res = dot_tn(xo[:, pl.ds(g * 512 + 384, 128)], cal[...]).astype(BF).reshape(2, 2, 2, 16, 1024)
@@ -745,28 +758,39 @@
 
     pairs_y = [at_y(d) for d in (1, 2, 3)] + [dev(z, x, y + d, 1 - c) for d in range(4)]
     plane_devices = [dev(z + dz, x + dx, y, c) for dz, dx in plane]
-    early, late = (sm, smr), (R["ln"], R["lnr"])
-
-    def exchange(level, slot, bufs, devices):
-        view = bufs[1].at[pl.ds(slot, len(devices))]
-        cps = Group(links, view, [(bufs[0].at[level], bufs[1].at[slot + d], t) for d, t in enumerate(devices)])
-        cps.start()
-        return cps
-
-    def plane_sum(bufs, cps):
-        cps.wait()
-        total = bufs[0][0]
-        for d in range(15):
-            total = total + bufs[1][d]
-        bufs[0][1] = total
-
-    def finish_sums(bufs, cps, out):
-        cps.wait()
-        same, other = bufs[0][1], bufs[1][18]
-        for d in range(3):
-            same = same + bufs[1][15 + d]
-            other = other + bufs[1][19 + d]
-        out[c], out[1 - c] = same, other
+    sp, spr, sq, sqr = (R[n] for n in ("sp", "spr", "sq", "sqr"))
+
+    def bias_plane():
+        row = [sm[0, r : r + 1, n * 256 : (n + 1) * 256] for r in (0, 1, 2, 4) for n in range(4)]
+        sp[0] = jnp.concatenate(row, axis=0).astype(BF)
+        group = Group(links, spr, [(sp.at[0], spr.at[n], d) for n, d in enumerate(plane_devices)])
+        group.start()
+        return group
+
+    def bias_chips(group):
+        group.wait()
+        row = [sm[0, r : r + 1, n * 256 : (n + 1) * 256] for r in (0, 1, 2, 4) for n in range(4)]
+        total = jnp.concatenate(row, axis=0)
+        for n in range(15):
+            total = total + spr[n].astype(F32)
+        sq[0] = total
+        group = Group(links, sqr, [(sq.at[0], sqr.at[n], d) for n, d in enumerate(pairs_y)])
+        group.start()
+        return group
+
+    def bias_done(group):
+        group.wait()
+        same = [(0, sq[0])] + [(d, sqr[d - 1]) for d in (1, 2, 3)]
+        other = [(d, sqr[3 + d]) for d in range(4)]
+        for core, parts in ((c, same), (1 - c, other)):
+            total = parts[0][1] + parts[1][1] + parts[2][1] + parts[3][1]
+            o_small[core, 0:8] = total[0:8]
+            o_small[core, 16:24] = total[8:16]
+            both = [jnp.zeros((4, 256), F32)] * 2
+            for d, val in parts:
+                at_high = ((y + 4 - d) % 4) // 2
+                both = [acc + jnp.where(at_high == h, val[8:12], 0.0) for h, acc in enumerate(both)]
+            o_small[core, 8:16] = jnp.concatenate(both, axis=0)
 
     def send_grad_mixed():
         for g in range(2):
@@ -783,20 +807,50 @@
         return cp
 
     def sum_strip(u, carry):
-        sg, sb = carry
         ru = pl.ds(pl.multiple_of(u * 32, 32), 32)
-        r = pl.ds(pl.multiple_of(mine_at + u * 32, 32), 32)
-        gn = gnp[r, :] + rxs[1, ru, :].astype(F32)
-        gnp[r, :] = gn
-        hat = (tokens[ru, :].astype(F32) - mr[0, ru, 0:1]) * mr[1, ru, 0:1]
-        return sg + jnp.sum((gn * hat).reshape(4, 8, D), axis=0), sb + jnp.sum(gn.reshape(4, 8, D), axis=0)
+        for at, tok, stat in ((mine_at, tokens, mr), (theirs_at, R["tsib"], R["msib"])):
+            gn = gnp[pl.ds(pl.multiple_of(at + u * 32, 32), 32), :]
+            hat = (tok[ru, :].astype(F32) - stat[0, ru, 0:1]) * stat[1, ru, 0:1]
+            carry = (carry[0] + jnp.sum((gn * hat).reshape(4, 8, D), axis=0), carry[1] + jnp.sum(gn.reshape(4, 8, D), axis=0))
+        return carry
+
+    ln, lnr, lnp, lnq = (R[n] for n in ("ln", "lnr", "lnp", "lnq"))
 
     def norm_sums():
         zero = jnp.zeros((8, D), F32)
-        for r, val in enumerate(lax.fori_loop(0, 8, sum_strip, (zero, zero), unroll=2)):
-            val = jnp.sum(val, axis=0, keepdims=True)
-            for n in range(4):
-                R["ln"][0, 4 * r + n : 4 * r + n + 1, :] = val[:, n * 256 : (n + 1) * 256]
+        sg, sb = (jnp.sum(v, axis=0, keepdims=True) for v in lax.fori_loop(0, 8, sum_strip, (zero, zero)))
+        low = lax.broadcasted_iota(jnp.int32, (1, 128), 1) < 64
+        for n in range(8):
+            g, b = sg[:, n * 128 : (n + 1) * 128], sb[:, n * 128 : (n + 1) * 128]
+            swap_g, swap_b = (jnp.concatenate([v[:, 64:128], v[:, 0:64]], axis=1) for v in (g, b))
+            ln[2 * n] = jnp.where(low, g, swap_b)
+            ln[2 * n + 1] = jnp.where(low, swap_g, b)
+
+    def norm_plane():
+        copies = []
+        for n, (dz, dx) in enumerate(plane):
+            place_of = ((z + dz) % 4) * 4 + (x + dx) % 4
+            copies.append((ln.at[place_of], lnr.at[n], dev(z + dz, x + dx, y, c)))
+        group = Group(links, lnr, copies)
+        group.start()
+        return group
+
+    def norm_chips(group):
+        group.wait()
+        total = ln[z * 4 + x]
+        for n in range(15):
+            total = total + lnr[n]
+        lnp[0] = total
+        group = Group(links, lnq, [(lnp.at[0], lnq.at[n], d) for n, d in enumerate(pairs_y)])
+        group.start()
+        return group
+
+    def norm_done(group):
+        group.wait()
+        total = lnp[0]
+        for n in range(7):
+            total = total + lnq[n]
+        o_ln[...] = total
 
     def last_strip(u, carry):
         ru = pl.ds(pl.multiple_of(u * 32, 32), 32)
@@ -806,7 +860,7 @@
         o_out[ru, :] = (xin + total + vecs[2:3, :] + vecs[3:4, :]).astype(BF)
         rs = mr[1, ru, 0:1]
         hat = (xin - mr[0, ru, 0:1]) * rs
-        n = gnp[r, :] * gain
+        n = (gnp[r, :] + rxs[1, ru, :].astype(F32)) * gain
         grad = n - jnp.mean(n, axis=-1, keepdims=True) - hat * jnp.mean(n * hat, axis=-1, keepdims=True)
         o_tok[ru, :] = cot[ru, :].astype(F32) + grad * rs
         return carry
@@ -858,83 +912,91 @@
         cp.wait_recv()
     red_b.step()
     attend(0, 3)
+    send_back(0, 3)
+    red_d.step()
     red_a.step()
     attend(0, 2)
-    red_d.step()
+    send_back(0, 2)
     attend(0, 1)
+    send_back(0, 1)
     attend(0, 0)
-    send_back(0)
+    send_back(0, 0)
+    cot_p.wait_recv()
+    cot_f = forward(cal)
     qkv_grads(0)
     red2 = reduce_qkv(0)
     red2.step()
+    red_c.step()
     attend(1, 3)
-    red_c.step()
+    send_back(1, 3)
     attend(1, 2)
+    send_back(1, 2)
+    red_e.step()
     attend(1, 1)
+    send_back(1, 1)
     attend(1, 0)
-    send_back(1)
-    red_e.step()
+    send_back(1, 0)
+    red_d.step()
     qkv_grads(1)
     red3 = reduce_qkv(1)
     red3.step()
-    red2.step()
-    cot_p.wait_recv()
-    cot_f = forward(cal)
     for g in range(2):
         bias_grads(g)
-    sums = exchange(0, 0, early, plane_devices)
+    sums = bias_plane()
+    red_a.step()
+    red_b.step()
+    red_e.step()
     cot_f.wait_recv()
     for g in range(2):
         out_grads(g)
     red4 = reduce_out()
     red4.step()
+    red2.step()
     red_d.step()
+    back[0].wait_recv()
+    outputs(0)
+    red_c.step()
+    red3.step()
+    outputs(1)
+    sums = bias_chips(sums)
     red_a.step()
     red_b.step()
-    back[0].wait_recv()
-    loop(2, outputs)
+    red4.step()
+    red2.step()
+    outputs(2)
     red_c.step()
+    red_d.step()
+    red_e.step()
+    outputs(3)
     red3.step()
     red4.step()
-    red2.step()
-    plane_sum(early, sums)
-    sums = exchange(1, 15, early, pairs_y)
-    red_e.step()
-    red_a.step()
     red_b.step()
-    loop(2, lambda n: outputs(n + 2))
-    red_d.step()
-    red_c.step()
-    red3.step()
-    red4.step()
-    red_e.step()
-    red_d.step()
-    red2.step()
-    red_b.step()
-    red_c.step()
-    finish_sums(early, sums, o_small)
+    bias_done(sums)
     back[1].wait_recv()
     project_last(theirs_at)
+    for cp in (tok_s, sta_s):
+        cp.wait_recv()
     loop(4, stage_strip)
     swap = [pieces(links, stage.at[pl.ds(w * 256, 256), :], rxs.at[w], sibling, PIECE) for w in range(2)]
     for cp in swap:
         cp.start()
+    red_e.step()
+    red_c.step()
+    red_d.step()
+    red2.step()
     project_last(mine_at)
-    red_e.step()
+    norm_sums()
+    sums = norm_plane()
     red3.step()
-    red_d.step()
+    red4.step()
     for cp in swap:
         cp.wait()
-    norm_sums()
-    sums = exchange(0, 0, late, plane_devices)
     lax.fori_loop(0, 8, last_strip, 0, unroll=2)
-    red4.step()
+    sums = norm_chips(sums)
     red_e.step()
-    plane_sum(late, sums)
-    sums = exchange(1, 15, late, pairs_y)
-    for cp in (cot_s, nrm_s, cot_p, nrm_p, cot_f, nrm_f):
+    for cp in (cot_s, nrm_s, cot_p, nrm_p, cot_f, nrm_f, tok_s, sta_s):
         cp.wait_send()
-    finish_sums(late, sums, o_ln)
+    norm_done(sums)
     for cp in back:
         cp.wait_send()
     links.whole(o_win.at[:, pl.ds(0, 2048)], *shared[0]).wait()
@@ -953,17 +1015,20 @@
     for src, dst in zip(raw, outs):
         dst[...] = src[...]
     index = lax.axis_index("dp") * 4 + lax.axis_index("seq")
-    for r in (3, 5):
-        line[r : r + 1, 0:D] = small[0, 4:5, :] + small[1, 4:5, :]
+    for n in range(4):
+        cols = pl.ds(n * 256, 256)
+        for r in (3, 5):
+            line[r : r + 1, cols] = small[0, 20 + n : 21 + n, :] + small[1, 20 + n : 21 + n, :]
+        for q in range(4):
+            line[4:5, pl.ds(q * 1024 + n * 256, 256)] = small[q % 2, 4 * (q // 2) + n : 4 * (q // 2) + n + 1, :]
+            if n < 3:
+                line[2:3, pl.ds(n * 1024 + q * 256, 256)] = small[q % 2, 8 + 4 * (q // 2) + n : 9 + 4 * (q // 2) + n, :]
     for r in range(2):
-        for n in range(4):
-            row = slice(4 * r + n, 4 * r + n + 1)
-            line[r : r + 1, n * 256 : (n + 1) * 256] = ln[0, row, :] + ln[1, row, :]
-    for t in range(4):
-        line[4:5, t * 1024 : (t + 1) * 1024] = small[t % 2, t // 2 : t // 2 + 1, :]
-        for j in range(3):
-            line[2:3, pl.ds(j * 1024 + t * 256, 256)] = small[t % 2, 2 + t // 2 : 3 + t // 2, j * 256 : (j + 1) * 256]
+        mine = pltpu.roll(jnp.broadcast_to(ln[...], (8, 128)), (128 - (index % 8) * 8 - 64 * r) % 128, 1)
+        vec[r][...] = mine[0, 0:8]
     for r, out in enumerate(vec):
+        if r < 2:
+            continue
         n = out.shape[0]
         at = index * n
         part = line[r : r + 1, pl.ds(pl.multiple_of((at // 128) * 128, 128), 256)]
@@ -985,8 +1050,8 @@
             sds((8, D), F32),
             sds((8, 4 * D), F32),
             sds((32, D), F32),
-            sds((2, 8, 1024), F32),
-            sds((2, 8, 256), F32),
+            sds((2, 24, 256), F32),
+            sds((1, 128), F32),
         ],
         in_specs=[V] * 6 + [S, V, V, H, H, H, H],
         out_specs=[V] * 8,

time: 102 us -> 94.1 us (0.923)
  Pallas kernels: 101 us -> 93.1 us
    pallas_call x1, Pallas kernels: 98.1 us -> 90.2 us  [on_device(): pl.pallas_call(kernel, out_shape=[sds((BLK, D), BF), sds((BLK, D), F32),...]
where the time goes in v5:
time: 94.1 us; the launch traced here: 93.9 us
  Pallas kernels  93.1 us (99%)
    pallas_call x1, Pallas kernels, on_device(): pl.pallas_call(kernel, out_shape=[sds((BLK, D), BF), sds((BLK, D), F32),...  90.2 us
    pallas_call x1, Pallas kernels, on_device(): pl.pallas_call(hand_over, out_shape=[sds(o.shape, o.dtype) for o in outs[...  2.91 us

profile of v5, /device:TPU:1, one launch (start us, length us, event | category | flops | bytes accessed | tf_op | source)
XLA Modules:
  0.0 93.9 jit_solution(783902785091281498)
XLA Ops:
  0.6 90.2 %layer.1 = (bf16[256,1024]{1,0:T(8,128)(2,1)}, f32[256,1024]{1,0:T(8,128)}, f32[8,3072]{1,0:T(8,128)}, f32[8,1024]{1,0:T(8,128)}, f32[8,4096]{1,0:T(8,128)}, /*i...) custom-call(bf16[1024]{0:T(1024)(128)(2,1)} %refs_0_.1, bf16[1024]{0:T(1024)(128)(2,1)} %refs_1_.1, ...), custom_call_target="tpu_custom_call" | custom-call | tf_op jit(solution)/shard_map/layer/pallas_call | solution.py:1044
  90.8 2.9 %shares.1 = (bf16[256,1024]{1,0:T(8,128)(2,1)}, f32[256,1024]{1,0:T(8,128)}, f32[8,3072]{1,0:T(8,128)}, f32[8,1024]{1,0:T(8,128)}, f32[8,4096]{1,0:T(8,128)}, /*...) custom-call(bf16[256,1024]{1,0:T(8,128)(2,1)} %get-tuple-element.32., ...), custom_call_target="tpu_custom_call" | custom-call | tf_op jit(solution)/shard_map/shares/pallas_call | solution.py:1064
